TPU v7x, 256 devices: a whole 4x4x8 slice. The times are simulated.
256 devices in a mesh: prow: 8 (over y, core), pcol: 32 (over x, z).
Axes of the slice: x: 4, y: 4, z: 8, core: 2. Of those that a mesh axis runs over, the one named last changes fastest.
Arguments:
- covariance: bfloat16 [8, 8, 256, 2, 32, 256], P(None, 'prow', None, None, 'pcol'), may hold values from 0 to 3, as said below
Outputs:
- factored: float32 [8, 8, 256, 2, 32, 256], P(None, 'prow', None, None, 'pcol')
Inputs may be any that keep to these rules, and one draw needn't show every extreme that they name: `covariance`: the matrix is symmetric and positive definite.
All inputs are finite; a program needn't handle non-finite values.
Results may differ from a plain program's by a relative error of at most 0.0003.
Values sent between devices are 32-bit elements; how exact they have to be, the bound alone decides.
A program may use at most 64 MiB of HBM per device.

v0:
```python
import jax
import jax.numpy as jnp
from jax import lax
from jax.sharding import PartitionSpec as P

PANELS = 4


def broadcast(shard, axis, root):
    mine = lax.axis_index(axis) == root
    return lax.psum(jnp.where(mine, shard, jnp.zeros_like(shard)), axis)


def small_factor(diag_tile, identity):
    factor = jnp.linalg.cholesky(diag_tile)
    inverse = lax.linalg.triangular_solve(factor, identity, left_side=True, lower=True)
    return (factor, inverse)


def solve_rows(column, inverse):
    return jnp.einsum(
        "rae,be->rab",
        column,
        inverse,
        precision=lax.Precision.HIGHEST,
        preferred_element_type=jnp.float32,
    )


def finish_panel(solved, factor, tile_rows, panel_index):
    below_mask = (tile_rows > panel_index)[:, None, None]
    diag_mask = (tile_rows == panel_index)[:, None, None]
    return jnp.where(below_mask, solved, jnp.where(diag_mask, factor[None, :, :], 0.0))


def local(covariance):
    prow_count = lax.axis_size("prow")
    pcol_count = lax.axis_size("pcol")
    my_row = lax.axis_index("prow")
    my_col = lax.axis_index("pcol")
    row_tiles = covariance.shape[0]
    tile_size = covariance.shape[2]
    col_tiles = covariance.shape[3]
    local_tiles = covariance.astype(jnp.float32).reshape(row_tiles, tile_size, col_tiles, tile_size)
    tile_rows = jnp.arange(row_tiles, dtype=jnp.int32) * prow_count + my_row
    tile_cols = jnp.arange(col_tiles, dtype=jnp.int32) * pcol_count + my_col
    identity = jnp.eye(tile_size, dtype=jnp.float32)
    next_source = None
    for panel_index in range(PANELS):
        root_row = panel_index % prow_count
        root_col = panel_index % pcol_count
        local_row = panel_index // prow_count
        local_col = panel_index // pcol_count
        column = local_tiles[:, :, local_col, :]
        diag_tile = broadcast(column[local_row], "prow", root_row)
        diag_tile = jnp.where(my_col == root_col, diag_tile, identity)
        factor, inverse = small_factor(diag_tile, identity)
        solved_panel = finish_panel(solve_rows(column, inverse), factor, tile_rows, panel_index)
        solved_panel = broadcast(solved_panel, "pcol", root_col)
        picked_rows = (jnp.arange(col_tiles, dtype=jnp.int32) * pcol_count + my_col) // prow_count
        mirrored = broadcast(
            jnp.take(solved_panel, picked_rows, axis=0), "prow", my_col % prow_count
        )
        row_panel = jnp.where((tile_rows > panel_index)[:, None, None], solved_panel, 0.0)
        col_panel = jnp.where((tile_cols > panel_index)[:, None, None], mirrored, 0.0)
        owner_column = jnp.where(my_col == root_col, solved_panel, column)
        local_tiles = local_tiles.at[:, :, local_col, :].set(owner_column)
        row_zero = (tile_rows == panel_index)[:, None, None, None] & (tile_cols > panel_index)[
            None, None, :, None
        ]
        local_tiles = jnp.where(row_zero, 0.0, local_tiles)
        update = jnp.einsum(
            "rae,cbe->racb",
            row_panel,
            col_panel,
            precision=lax.Precision.HIGHEST,
            preferred_element_type=jnp.float32,
        )
        local_tiles = local_tiles - update
        next_source = None
    return local_tiles.reshape(row_tiles, 1, tile_size, col_tiles, 1, tile_size)


def solution(mesh):
    in_specs = (P(None, "prow", None, None, "pcol", None),)
    out_specs = P(None, "prow", None, None, "pcol", None)
    return jax.shard_map(local, mesh=mesh, in_specs=in_specs, out_specs=out_specs, check_vma=False)
```

profile of v0, /device:TPU:9, one launch (start us, length us, event | category | flops | bytes accessed | tf_op | source)
XLA Modules:
  0.0 1469.1 jit_solution(1299480163326263265)
XLA Ops:
  6.5 4.7 copy.2
  15.5 63.7 %all-reduce.14.cloned.1.call-done = f32[256,256]{0,1:T(8,128)} async-done(((f32[256,256]{0,1:T(8,128)}), f32[256,256]{0,1:T(8,128)}) %all-reduce.14.cloned.1.call-update) | async-done | bytes 262160 | tf_op jit(solution)/shard_map/psum | solution.py:11
  81.3 11.7 cholesky.214
  93.1 9.8 custom-call.17
  103.4 11.7 cholesky.231
  117.2 4.2 while.12
  121.5 19.7 %custom-call.18 = f32[2,128,128]{1,2,0:T(8,128)S(1)} custom-call(f32[2,128,128]{2,1,0:T(8,128)S(1)} %get-tuple-element.82), custom_call_target="InvertDiagBlocksLowerTriangular" | custom-call | tf_op jit(solution)/shard_map/triangular_solve/custom-call.0 | solution.py:16
  145.0 151.2 %all-reduce.16.cloned.1.call-done = f32[8,256,256]{1,2,0:T(8,128)} async-done(((f32[8,256,256]{1,2,0:T(8,128)}), f32[8,256,256]{1,2,0:T(8,128)}) %all-reduce.16.cloned.1.call-update) | async-done | bytes 2097168 | tf_op jit(solution)/shard_map/psum | solution.py:11
  299.6 3.2 fusion.2
  302.8 60.1 %all-reduce.18.cloned.1.call-done = f32[2,256,256]{1,2,0:T(8,128)} async-done(((f32[2,256,256]{1,2,0:T(8,128)}), f32[2,256,256]{1,2,0:T(8,128)}) %all-reduce.18.cloned.1.call-update) | async-done | bytes 524304 | tf_op jit(solution)/shard_map/psum | solution.py:11
  362.8 6.3 select_subtract_fusion.2
  372.1 64.1 %all-reduce.20.cloned.1.call-done = f32[256,256]{0,1:T(8,128)} async-done(((f32[256,256]{0,1:T(8,128)}), f32[256,256]{0,1:T(8,128)}) %all-reduce.20.cloned.1.call-update) | async-done | bytes 262160 | tf_op jit(solution)/shard_map/psum | solution.py:11
  436.5 11.7 cholesky.248
  448.3 9.8 custom-call.19
  458.6 11.7 cholesky.265
  473.0 4.3 while.13
  477.3 19.7 %custom-call.20 = f32[2,128,128]{1,2,0:T(8,128)S(1)} custom-call(f32[2,128,128]{2,1,0:T(8,128)S(1)} %get-tuple-element.83), custom_call_target="InvertDiagBlocksLowerTriangular" | custom-call | tf_op jit(solution)/shard_map/triangular_solve/custom-call.0 | solution.py:16
  498.2 5.0 select_select_fusion.2
  503.4 3.0 slice_bitcast_fusion.2
  506.4 150.1 %all-reduce.22.cloned.1.call-done = f32[8,256,256]{1,2,0:T(8,128)} async-done(((f32[8,256,256]{1,2,0:T(8,128)}), f32[8,256,256]{1,2,0:T(8,128)}) %all-reduce.22.cloned.1.call-update) | async-done | bytes 2097168 | tf_op jit(solution)/shard_map/psum | solution.py:11
  659.8 3.2 bitcast_dynamic-update-slice_fusion.6
  663.0 60.1 %all-reduce.24.cloned.1.call-done = f32[2,256,256]{1,2,0:T(8,128)} async-done(((f32[2,256,256]{1,2,0:T(8,128)}), f32[2,256,256]{1,2,0:T(8,128)}) %all-reduce.24.cloned.1.call-update) | async-done | bytes 524304 | tf_op jit(solution)/shard_map/psum | solution.py:11
  723.1 6.3 select_subtract_fusion.1
  732.6 63.8 %all-reduce.26.cloned.1.call-done = f32[256,256]{0,1:T(8,128)} async-done(((f32[256,256]{0,1:T(8,128)}), f32[256,256]{0,1:T(8,128)}) %all-reduce.26.cloned.1.call-update) | async-done | bytes 262160 | tf_op jit(solution)/shard_map/psum | solution.py:11
  796.7 11.7 cholesky.282
  808.5 9.8 custom-call.21
  818.8 11.7 cholesky.299
  833.2 4.2 while.14
  837.4 19.7 %custom-call.22 = f32[2,128,128]{1,2,0:T(8,128)S(1)} custom-call(f32[2,128,128]{2,1,0:T(8,128)S(1)} %get-tuple-element.84), custom_call_target="InvertDiagBlocksLowerTriangular" | custom-call | tf_op jit(solution)/shard_map/triangular_solve/custom-call.0 | solution.py:16
  858.3 5.0 select_select_fusion.1
  863.5 4.5 copy.25
  868.0 148.7 %all-reduce.28.cloned.1.call-done = f32[8,256,256]{1,2,0:T(8,128)} async-done(((f32[8,256,256]{1,2,0:T(8,128)}), f32[8,256,256]{1,2,0:T(8,128)}) %all-reduce.28.cloned.1.call-update) | async-done | bytes 2097168 | tf_op jit(solution)/shard_map/psum | solution.py:11
  1020.0 3.3 bitcast_dynamic-update-slice_fusion.5
  1023.3 60.0 %all-reduce.30.cloned.1.call-done = f32[2,256,256]{1,2,0:T(8,128)} async-done(((f32[2,256,256]{1,2,0:T(8,128)}), f32[2,256,256]{1,2,0:T(8,128)}) %all-reduce.30.cloned.1.call-update) | async-done | bytes 524304 | tf_op jit(solution)/shard_map/psum | solution.py:11
  1083.2 6.3 select_subtract_fusion
  1092.6 64.1 %all-reduce.32.cloned.1.call-done = f32[256,256]{0,1:T(8,128)} async-done(((f32[256,256]{0,1:T(8,128)}), f32[256,256]{0,1:T(8,128)}) %all-reduce.32.cloned.1.call-update) | async-done | bytes 262160 | tf_op jit(solution)/shard_map/psum | solution.py:11
  1156.9 11.7 cholesky.316
  1168.7 9.8 custom-call.23
  1179.0 11.7 cholesky.333
  1193.4 4.3 while.15
  1197.7 19.7 %custom-call.24 = f32[2,128,128]{1,2,0:T(8,128)S(1)} custom-call(f32[2,128,128]{2,1,0:T(8,128)S(1)} %get-tuple-element.85), custom_call_target="InvertDiagBlocksLowerTriangular" | custom-call | tf_op jit(solution)/shard_map/triangular_solve/custom-call.0 | solution.py:16
  1218.5 5.0 select_select_fusion
  1223.8 3.0 slice_bitcast_fusion
  1226.8 150.1 %all-reduce.34.cloned.1.call-done = f32[8,256,256]{1,2,0:T(8,128)} async-done(((f32[8,256,256]{1,2,0:T(8,128)}), f32[8,256,256]{1,2,0:T(8,128)}) %all-reduce.34.cloned.1.call-update) | async-done | bytes 2097168 | tf_op jit(solution)/shard_map/psum | solution.py:11
  1380.2 3.2 bitcast_dynamic-update-slice_fusion.4
  1383.4 60.1 %all-reduce.36.cloned.1.call-done = f32[2,256,256]{1,2,0:T(8,128)} async-done(((f32[2,256,256]{1,2,0:T(8,128)}), f32[2,256,256]{1,2,0:T(8,128)}) %all-reduce.36.cloned.1.call-update) | async-done | bytes 524304 | tf_op jit(solution)/shard_map/psum | solution.py:11
  1443.5 7.5 subtract_bitcast_fusion
  1451.0 10.9 copy.38
  (161 shorter events, 60.4 us)
Async XLA Ops:
  6.5 72.6 %all-reduce.14.cloned.1.call-start = ((), (), s32[]{:S(2)}) async-start(), calls=%async_computation | async-start | bytes 524288 | tf_op jit(solution)/shard_map/psum | solution.py:11
  15.4 280.9 %all-reduce.16.cloned.1.call-start = ((), (), s32[]{:S(2)}) async-start(), calls=%async_computation.1 | async-start | bytes 4194304 | tf_op jit(solution)/shard_map/psum | solution.py:11
  144.8 218.0 %all-reduce.18.cloned.1.call-start = ((), (), s32[]{:S(2)}) async-start(), calls=%async_computation.2 | async-start | bytes 1048576 | tf_op jit(solution)/shard_map/psum | solution.py:11
  296.2 3.3 copy-start.3
  299.5 136.7 %all-reduce.20.cloned.1.call-start = ((), (), s32[]{:S(2)}) async-start(), calls=%async_computation.3 | async-start | bytes 524288 | tf_op jit(solution)/shard_map/psum | solution.py:11
  369.1 2.0 copy-start.2
  371.8 284.6 %all-reduce.22.cloned.1.call-start = ((), (), s32[]{:S(2)}) async-start(), calls=%async_computation.4 | async-start | bytes 4194304 | tf_op jit(solution)/shard_map/psum | solution.py:11
  503.2 219.9 %all-reduce.24.cloned.1.call-start = ((), (), s32[]{:S(2)}) async-start(), calls=%async_computation.5 | async-start | bytes 1048576 | tf_op jit(solution)/shard_map/psum | solution.py:11
  656.5 3.3 copy-start.5
  659.8 136.7 %all-reduce.26.cloned.1.call-start = ((), (), s32[]{:S(2)}) async-start(), calls=%async_computation.6 | async-start | bytes 524288 | tf_op jit(solution)/shard_map/psum | solution.py:11
  729.4 2.0 copy-start.1
  732.1 284.6 %all-reduce.28.cloned.1.call-start = ((), (), s32[]{:S(2)}) async-start(), calls=%async_computation.7 | async-start | bytes 4194304 | tf_op jit(solution)/shard_map/psum | solution.py:11
  863.4 219.9 %all-reduce.30.cloned.1.call-start = ((), (), s32[]{:S(2)}) async-start(), calls=%async_computation.8 | async-start | bytes 1048576 | tf_op jit(solution)/shard_map/psum | solution.py:11
  1016.7 3.3 copy-start.6
  1020.0 136.7 %all-reduce.32.cloned.1.call-start = ((), (), s32[]{:S(2)}) async-start(), calls=%async_computation.9 | async-start | bytes 524288 | tf_op jit(solution)/shard_map/psum | solution.py:11
  1089.5 2.0 copy-start
  1092.3 284.6 %all-reduce.34.cloned.1.call-start = ((), (), s32[]{:S(2)}) async-start(), calls=%async_computation.10 | async-start | bytes 4194304 | tf_op jit(solution)/shard_map/psum | solution.py:11
  1223.6 219.9 %all-reduce.36.cloned.1.call-start = ((), (), s32[]{:S(2)}) async-start(), calls=%async_computation.11 | async-start | bytes 1048576 | tf_op jit(solution)/shard_map/psum | solution.py:11
  1376.9 3.3 copy-start.4
Sparse Core Ops, SparseCore 0:
  15.5 63.6 all-reduce.13
  144.9 151.2 all-reduce.15
  299.6 63.1 all-reduce.17
  372.0 64.2 all-reduce.19
  503.3 153.1 all-reduce.21
  659.9 63.1 all-reduce.23
  732.2 64.1 all-reduce.25
  863.5 153.1 all-reduce.27
  1020.1 63.1 all-reduce.29
  1092.4 64.2 all-reduce.31
  1223.7 153.1 all-reduce.33
  1380.3 63.1 all-reduce.35
where the time goes:
time: 1480 us; the launch traced here: 1470 us
  waiting for transfers between devices  1100 us (74%)
  other arithmetic  242 us (16%)
  local copies, waits for them, and re-layouts  58.7 us (4%)
  matrix products  49.7 us (3%)
  between operations  19.7 us (1%)
    psum x12, waiting for transfers between devices, broadcast(): return lax.psum(jnp.where(mine, shard, jnp.zeros_like(shard)), axis)  1100 us
    another operation x27, other arithmetic, small_factor(): factor = jnp.linalg.cholesky(diag_tile)  138 us
    another operation x9, other arithmetic, small_factor(): lax.linalg.triangular_solve(factor, identity, left_side=True, lower=True)  78.8 us
  transfers between devices with their start and end apart: 12, of which 12 were waited for; matrix products, arithmetic and copies ran while one was open for 2% of the time, Pallas kernels for 0%

commit v1 on v0

v1 whole, which is shorter than its diff:
```python
import functools
import jax
import jax.numpy as jnp
from jax import lax
from jax.experimental import pallas as pl
from jax.experimental.pallas import tpu as pltpu
from jax.sharding import PartitionSpec as P

B = 256
NP = 4
TOP = NP * B
F32 = jnp.float32
BF16 = jnp.bfloat16
MESH = pl.DeviceIdType.MESH


def split(a):
    hi = a.astype(BF16)
    return hi, (a - hi.astype(F32)).astype(BF16)


def dot1(a, b):
    return jnp.dot(a, b, preferred_element_type=F32)


def dot3(a, b):
    ah, al = split(a)
    bh, bl = split(b)
    return dot1(ah, bh) + (dot1(ah, bl) + dot1(al, bh))


def spread_kernel(a_ref, m_ref, g_ref, rg, rm, so, sf, st):
    p = lax.axis_index("prow")
    q = lax.axis_index("pcol")
    x = q // 8
    z = q % 8
    par = p % 2
    sib = p + 1 - 2 * par

    barrier = pltpu.get_barrier_semaphore()
    partners = [(lax.rem(p + d, 8), q) for d in range(1, 8)]
    partners += [(p, lax.rem(q + 8 * d, 32)) for d in (1, 2, 3)]
    partners += [(p, 8 * x + lax.rem(z + d, 8)) for d in (1, 7)]
    for pp, qq in partners:
        pl.semaphore_signal(barrier, inc=1, device_id=(pp, qq), device_id_type=MESH)
    pl.semaphore_wait(barrier, len(partners))

    def send(src, dst, ssem, rsem, pp, qq):
        return pltpu.make_async_remote_copy(
            src_ref=src, dst_ref=dst, send_sem=ssem, recv_sem=rsem,
            device_id=(pp, qq), device_id_type=MESH,
        )

    def gslot(k, c):
        return g_ref.at[pl.ds(pl.multiple_of(k * B, B), B), pl.ds(c * B, B)]

    def mslot(k, kc):
        return m_ref.at[pl.ds(pl.multiple_of(k * B, B), B), pl.ds(kc * B, B)]

    def origin(c):
        for n, d in enumerate((2, 6, 4, None)):
            pp = sib if d is None else lax.rem(p + d, 8)
            yield send(a_ref.at[c], gslot(p, c), so.at[c, n], rg.at[p, c], pp, q)

    def relay(k, c):
        return send(gslot(k, c), gslot(k, c), sf.at[k, c], rg.at[k, c], sib, q)

    def strips(c):
        @pl.when(p < NP)
        def _():
            for cp in origin(c):
                cp.start()
            g_ref[pl.ds(pl.multiple_of(p * B, B), B), c * B:(c + 1) * B] = a_ref[c]
        for i in range(2):
            k = par + 2 * i

            @pl.when(k != p)
            def _():
                relay(k, c).wait_recv()
                relay(k, c).start()

    def tile_sends(i, kc):
        k = par + 2 * i
        d = lax.rem(z + 8 - kc, 8)
        slot = mslot(k, kc)
        rsem = rm.at[k, kc]
        out = []
        for n in range(3):
            out.append(((d == 0) & (x == 0),
                        send(slot, slot, st.at[i, kc, n], rsem, p, lax.rem(q + 8 * (n + 1), 32))))
        out.append((d < 4, send(slot, slot, st.at[i, kc, 3], rsem, p, 8 * x + lax.rem(z + 1, 8))))
        out.append(((d == 0) | (d > 5), send(slot, slot, st.at[i, kc, 4], rsem, p, 8 * x + lax.rem(z + 7, 8))))
        out.append((None, send(slot, slot, st.at[i, kc, 5], rsem, sib, q)))
        return d, out

    strips(0)
    for i in range(2):
        for kc in range(NP):
            k = par + 2 * i

            @pl.when(k <= kc)
            def _():
                d, sends = tile_sends(i, kc)
                here = (d == 0) & (x == 0)

                @pl.when(here)
                def _():
                    rows = pl.ds(pl.multiple_of(k * B, B), B)
                    m_ref[rows, kc * B:(kc + 1) * B] = g_ref[rows, 0:B]

                @pl.when(jnp.logical_not(here))
                def _():
                    sends[5][1].wait_recv()
                for cond, cp in sends:
                    if cond is None:
                        cp.start()
                    else:
                        pl.when(cond)(cp.start)
    strips(1)

    for i in range(2):
        k = 1 - par + 2 * i
        for c in range(2):
            relay(k, c).wait_recv()
        for kc in range(NP):
            @pl.when(k <= kc)
            def _():
                slot = mslot(k, kc)
                send(slot, slot, st.at[i, kc, 5], rm.at[k, kc], sib, q).wait_recv()

    for c in range(2):
        @pl.when(p < NP)
        def _():
            for cp in origin(c):
                cp.wait_send()
        for i in range(2):
            k = par + 2 * i

            @pl.when(k != p)
            def _():
                relay(k, c).wait_send()
    for i in range(2):
        for kc in range(NP):
            @pl.when(par + 2 * i <= kc)
            def _():
                for cond, cp in tile_sends(i, kc)[1]:
                    if cond is None:
                        cp.wait_send()
                    else:
                        pl.when(cond)(cp.wait_send)


def spread(a):
    dma = pltpu.SemaphoreType.DMA
    return pl.pallas_call(
        spread_kernel,
        out_shape=(jax.ShapeDtypeStruct((TOP, TOP), F32), jax.ShapeDtypeStruct((TOP, 2 * B), F32)),
        in_specs=[pl.BlockSpec(memory_space=pltpu.VMEM)],
        out_specs=[pl.BlockSpec(memory_space=pltpu.VMEM)] * 2,
        scratch_shapes=[dma((NP, 2)), dma((NP, NP)), dma((2, 4)), dma((NP, 2)), dma((2, NP, 6))],
        compiler_params=pltpu.CompilerParams(
            collective_id=1, has_side_effects=True, vmem_limit_bytes=32 * 1024 * 1024),
        name="spread",
    )(a)


def panel(R, j, sub, lane):
    for g in range(4):
        c0 = j + 8 * g
        lt = c0 // 128
        o = c0 % 128
        cb = {}
        for h in range(g, 4):
            for t in range(8):
                cb[h, t] = jnp.broadcast_to(R[h][lt][:, o + t:o + t + 1], (8, 128))
        inblk = (lane >= o) & (lane < o + 8)
        R[g][lt] = jnp.where(inblk, jnp.where(lane - o == sub, 1.0, 0.0), R[g][lt])
        for h in range(g + 1, 4):
            R[h][lt] = jnp.where(inblk, 0.0, R[h][lt])
        scale = jnp.zeros((8, 128), F32)
        for t in range(8):
            piv = jnp.broadcast_to(cb[g, t][t:t + 1, :], (8, 128))
            inv = 1.0 / piv
            scale = jnp.where(sub == t, lax.rsqrt(piv), scale)
            rows = [jnp.broadcast_to(R[g][l][t:t + 1, :], (8, 128)) for l in range(2)]
            crow = {u: jnp.broadcast_to(cb[g, u][t:t + 1, :], (8, 128)) for u in range(t + 1, 8)}
            for h in range(g, 4):
                f = cb[h, t] * inv
                if h == g:
                    f = jnp.where(sub > t, f, 0.0)
                for l in range(2):
                    R[h][l] = R[h][l] - f * rows[l]
                for u in range(t + 1, 8):
                    cb[h, u] = cb[h, u] - f * crow[u]
        for u in range(1, 8):
            R[g][lt] = jnp.where((lane == o + u) & (sub < u), cb[g, u], R[g][lt])
        for l in range(2):
            R[g][l] = R[g][l] * scale
    return R


def factor_tile(T):
    sub = lax.broadcasted_iota(jnp.int32, (8, 128), 0)
    lane = lax.broadcasted_iota(jnp.int32, (8, 128), 1)
    pr = lax.broadcasted_iota(jnp.int32, (32, B), 0)
    pc = lax.broadcasted_iota(jnp.int32, (32, B), 1)
    for jb in range(8):
        j = 32 * jb
        R = [[T[j + 8 * g:j + 8 * g + 8, 128 * l:128 * l + 128] for l in range(2)] for g in range(4)]
        R = panel(R, j, sub, lane)
        rows = jnp.concatenate([jnp.concatenate(r, axis=1) for r in R], axis=0)
        T[j:j + 32, :] = rows
        if jb < 7:
            left = rows.T[j + 32:, :]
            n = B - j - 32
            ln = lax.broadcasted_iota(jnp.int32, (n, B), 1)
            low = jnp.where((ln >= j) & (ln < j + 32), 0.0, T[j + 32:, :])
            rows = jnp.where((pc < j + 32) & (pc > j + pr), 0.0, rows)
            T[j + 32:, :] = low - dot3(left, rows)


def factor_kernel(m_ref, g_ref, whi_ref, wlo_ref, l_ref, S, T, W):
    p = lax.axis_index("prow")
    q = lax.axis_index("pcol")
    S[:, 0:TOP] = m_ref[...]
    S[:, TOP:TOP + 2 * B] = g_ref[...]
    row = lax.broadcasted_iota(jnp.int32, (B, B), 0)
    col = lax.broadcasted_iota(jnp.int32, (B, B), 1)

    def tile(i):
        return pl.ds(pl.multiple_of(i * B, B), B)

    def step(k, _):
        T[...] = S[tile(k), tile(k)]
        factor_tile(T)
        S[tile(k), tile(k)] = T[...]
        X = jnp.where(row >= col, T[...], 0.0)

        def solve(m, _):
            S[tile(k), tile(m)] = dot3(X, S[tile(k), tile(m)])
            return 0

        lax.fori_loop(k + 1, NP + 2, solve, 0)

        def trail(i, _):
            left = S[tile(k), tile(i)].T

            def inner(m, _):
                S[tile(i), tile(m)] = S[tile(i), tile(m)] - dot3(left, S[tile(k), tile(m)])
                return 0

            lax.fori_loop(i, NP + 2, inner, 0)
            return 0

        lax.fori_loop(k + 1, NP, trail, 0)
        return 0

    lax.fori_loop(0, NP, step, 0)

    kq = jnp.minimum(q, NP - 1)
    kp = jnp.minimum(p, NP - 1)
    u = S[tile(kq), tile(kp)]
    u_diag = jnp.where(col > row, u, jnp.where(col == row, 1.0 / u, 0.0))
    u = jnp.where(kp == kq, u_diag, jnp.where(kq < kp, u, 0.0))
    l_ref[...] = u.T

    col2 = lax.broadcasted_iota(jnp.int32, (B, 2 * B), 1)
    row2 = lax.broadcasted_iota(jnp.int32, (B, 2 * B), 0)
    for k in (3, 2, 1, 0):
        unit = jnp.where((row2 == col2) & (q == k), 1.0, 0.0)
        acc = jnp.where((col2 < B) & (q < NP), unit, S[k * B:(k + 1) * B, TOP:TOP + 2 * B])
        for m in range(k + 1, NP):
            acc = acc - dot3(S[k * B:(k + 1) * B, m * B:(m + 1) * B], W[m * B:(m + 1) * B, :])
        X = jnp.where(row >= col, S[k * B:(k + 1) * B, k * B:(k + 1) * B], 0.0)
        w = dot3(X.T, acc)
        W[k * B:(k + 1) * B, :] = w
        hi, lo = split(w)
        whi_ref[k * B:(k + 1) * B, :] = hi
        wlo_ref[k * B:(k + 1) * B, :] = lo


def factor(m11, g):
    vmem = pl.BlockSpec(memory_space=pltpu.VMEM)
    return pl.pallas_call(
        factor_kernel,
        out_shape=(
            jax.ShapeDtypeStruct((TOP, 2 * B), BF16),
            jax.ShapeDtypeStruct((TOP, 2 * B), BF16),
            jax.ShapeDtypeStruct((B, B), F32),
        ),
        in_specs=[vmem, vmem],
        out_specs=[vmem, vmem, vmem],
        scratch_shapes=[
            pltpu.VMEM((TOP, TOP + 2 * B), F32),
            pltpu.VMEM((B, B), F32),
            pltpu.VMEM((TOP, 2 * B), F32),
        ],
        compiler_params=pltpu.CompilerParams(vmem_limit_bytes=40 * 1024 * 1024),
        cost_estimate=pl.CostEstimate(
            flops=60_000_000_000, bytes_accessed=8_000_000, transcendentals=0),
        name="factor",
    )(m11, g)


def update_kernel(b_ref, m_ref, whi_ref, wlo_ref, l_ref, o_ref):
    r = pl.program_id(0)
    p = lax.axis_index("prow")
    q = lax.axis_index("pcol")
    acc = jnp.zeros((B, 2 * B), F32)
    for k in range(NP):
        left = b_ref[k].astype(BF16)
        acc = acc + dot1(left, whi_ref[k * B:(k + 1) * B, :])
        acc = acc + dot1(left, wlo_ref[k * B:(k + 1) * B, :])
    m = m_ref[0].astype(F32)
    top = (r == 0) & (p < NP)
    factor_col = q < NP
    c0 = jnp.where(factor_col, acc[:, 0:B], m[:, 0:B] - acc[:, 0:B])
    c0 = jnp.where(top, jnp.where(factor_col, l_ref[...], 0.0), c0)
    c1 = jnp.where(top, 0.0, m[:, B:] - acc[:, B:])
    for n, part in enumerate((c0[:, :128], c0[:, 128:], c1[:, :128], c1[:, 128:])):
        o_ref[pl.ds(n, B, stride=4), :] = part


def update(bulk, mine, whi, wlo, ltile):
    return pl.pallas_call(
        update_kernel,
        grid=(8,),
        out_shape=jax.ShapeDtypeStruct((8 * 4 * B, 128), F32),
        in_specs=[
            pl.BlockSpec((4, B, B), lambda r: (2 * (r % 4) + r // 4, 0, 0)),
            pl.BlockSpec((1, B, 2 * B), lambda r: (r, 0, 0)),
            pl.BlockSpec((TOP, 2 * B), lambda r: (0, 0)),
            pl.BlockSpec((TOP, 2 * B), lambda r: (0, 0)),
            pl.BlockSpec((B, B), lambda r: (0, 0)),
        ],
        out_specs=pl.BlockSpec((4 * B, 128), lambda r: (r, 0)),
        compiler_params=pltpu.CompilerParams(vmem_limit_bytes=32 * 1024 * 1024),
        cost_estimate=pl.CostEstimate(
            flops=4_300_000_000, bytes_accessed=16_000_000, transcendentals=0),
        name="update",
    )(bulk, mine, whi, wlo, ltile)


def local(covariance):
    mine = covariance.reshape(8, B, 2, B)
    strip = mine[0].astype(F32)
    a = strip.transpose(1, 0, 2)
    at = strip.transpose(1, 2, 0)
    mine = mine.reshape(8, B, 2 * B)
    tile = jnp.zeros((B, B), F32)
    for c in range(2):
        perm = [
            (k * 32 + 8 * x + z, z * 32 + 8 * x + 4 * c + k)
            for k in range(NP) for x in range(4) for z in range(8)
        ]
        tile = tile + lax.ppermute(at[c], ("prow", "pcol"), perm)
    bulk = lax.all_gather(tile, "pcol")
    m11, g = spread(a)
    whi, wlo, ltile = factor(m11, g)
    out = update(bulk, mine, whi, wlo, ltile)
    return out.reshape(8, 1, B, 2, 1, B)


def solution(mesh):
    in_specs = (P(None, "prow", None, None, "pcol", None),)
    out_specs = P(None, "prow", None, None, "pcol", None)
    return jax.shard_map(local, mesh=mesh, in_specs=in_specs, out_specs=out_specs, check_vma=False)
```

time: 1480 us -> 233 us (0.16)
  the two profiles are of different devices: /device:TPU:9 before, /device:TPU:245 now
where the time goes in v1:
time: 233 us
  Pallas kernels  176 us (76%)
  waiting for transfers between devices  21.9 us (9%)
  local copies, waits for them, and re-layouts  18.9 us (8%)
  between operations  13.5 us (6%)
    pallas_call x1, Pallas kernels, spread(): pl.pallas_call(spread_kernel, out_shape=(jax.ShapeDtypeStruct((TOP, TOP),...  122 us
    pallas_call x1, Pallas kernels, factor(): pl.pallas_call(factor_kernel, out_shape=(jax.ShapeDtypeStruct((TOP, 2 * B...  47.2 us
    ppermute x2, waiting for transfers between devices, local(): tile = tile + lax.ppermute(at[c], ('prow', 'pcol'), perm)  21.9 us
    all_gather x1, local copies, waits for them, and re-layouts, local(): bulk = lax.all_gather(tile, 'pcol')  8.97 us
    pallas_call x1, Pallas kernels, update(): pl.pallas_call(update_kernel, grid=(8,), out_shape=jax.ShapeDtypeStruct((...  6.71 us
    unnamed x6, local copies, waits for them, and re-layouts  5.57 us
  transfers between devices with their start and end apart: 3, of which 1 were waited for; matrix products, arithmetic and copies ran while one was open for 1% of the time, Pallas kernels for 73%

profile of v1, /device:TPU:245, one launch (start us, length us, event | category | flops | bytes accessed | tf_op | source)
XLA Modules:
  0.0 232.7 jit_solution(14615535504166460996)
XLA Ops:
  6.5 0.0 all-gather.3.cloned.1.call-start
  6.5 1.1 slice.10
  7.7 0.1 convert_bitcast_fusion
  7.8 0.7 collective-permute-start
  8.5 1.3 collective-permute-start.1
  9.8 0.0 collective-permute-done
  9.8 21.9 %collective-permute-done.1 = f32[256,256]{0,1:T(8,128)S(1)} collective-permute-done((f32[256,256]{0,1:T(8,128)S(1)}, f32[256,256]{0,1:T(8,128)S(1)}, u32[]{:S(2)}, u32[]{:S(2)}) %collective-permute-start.1) | collective-permute-done | bytes 262176 | tf_op jit(solution)/shard_map/ppermute | solution.py:356
  31.7 0.8 add.3
  32.4 0.0 all-gather.3.cloned.1.call-update
  32.4 3.2 %reshape_reshape.3.m_ref = bf16[8,256,512]{2,1,0:T(8,128)(2,1)S(1)} reshape(bf16[8,1,256,2,1,256]{5,3,4,2,1,0:T(2,128)(2,1)} %param.1) | data formatting | bytes 4194304 | tf_op jit(solution)/shard_map/reshape;reshape | solution.py:349
  35.6 121.7 %spread.1 = (f32[1024,1024]{1,0:T(8,128)S(1)}, f32[1024,512]{1,0:T(8,128)S(1)}) custom-call(f32[2,256,256]{2,1,0:T(8,128)S(1)} %get-tuple-element.17.a_ref), custom_call_target="tpu_custom_call" | custom-call | tf_op jit(solution)/shard_map/spread/pallas_call | solution.py:155
  157.3 47.2 %factor.1 = (bf16[1024,512]{1,0:T(8,128)(2,1)S(1)}, bf16[1024,512]{1,0:T(8,128)(2,1)S(1)}, f32[256,256]{1,0:T(8,128)S(1)}) custom-call(f32[1024,1024]{1,0:T(8,128)S(1)} %get-tuple-element.10.m_ref, f32[1024,512]{1,0:T(8,128)S(1)} %get-tuple-element.11.g_ref), custom_call_target="tpu_custom_call" | custom-call | flops 60000002048 | bytes 8000000 | tf_op jit(solution)/shard_map/factor/pallas_call | solution.py:284
  204.6 0.0 copy-start.1
  204.6 1.0 copy-done.1
  205.5 0.0 all-gather.3.cloned.1.call-done
  205.5 9.0 %copy.3 = f32[8192,256]{1,0:T(8,128)} copy(f32[8192,256]{0,1:T(8,128)} %all-gather.3.cloned.1.call-done) | data formatting | bytes 16777216 | tf_op jit(solution)/shard_map/all_gather | solution.py:357
  214.5 0.0 copy-start
  214.5 3.4 %copy-done = f32[8192,256]{1,0:T(8,128)S(1)} copy-done((f32[8192,256]{1,0:T(8,128)S(1)}, f32[8192,256]{1,0:T(8,128)}, u32[]{:S(2)}) %copy-start) | copy-done | bytes 8388632
  217.9 0.0 copy-start.2
  217.9 1.2 copy-done.2
  219.1 6.7 %update.1 = f32[8192,128]{1,0:T(8,128)} custom-call(f32[32,256,256]{2,1,0:T(8,128)S(1)} %bitcast.19, bf16[8,256,512]{2,1,0:T(8,128)(2,1)S(1)} %reshape_reshape.3.m_ref, bf16[1024,512]{1,0:T(8,128)(2,1)S(1)} %get-tuple-element.12.whi_ref, bf16[1024,512]{1,0:T(8,128)(2,1)S(1)} %copy-done.2, f32[256,256]{1,0:T(8,128)S(1)} %get-tuple-element.14.l_ref), custom_call_target="tpu_custom_call" | custom-call | flops 4300000256 | bytes 16000000 | tf_op jit(solution)/shard_map/update/pallas_call | solution.py:325
  (1 shorter events, 0.0 us)
Async XLA Ops:
  6.5 199.0 %all-gather.3.cloned.1.call-start = ((), (), s32[]{:S(2)}) async-start(), calls=%async_computation | async-start | bytes 8650752 | tf_op jit(solution)/shard_map/all_gather | solution.py:357
  7.8 2.0 collective-permute-start
  8.5 23.2 %collective-permute-start.1 = (f32[256,256]{0,1:T(8,128)S(1)}, f32[256,256]{0,1:T(8,128)S(1)}, u32[]{:S(2)}, u32[]{:S(2)}) collective-permute-start(f32[256,256]{0,1:T(8,128)S(1)} %get-tuple-element.15), channel_id=1, source_target_pairs={{0,4},{1,36},{2,68},{3,100},{4,132},{5,164},{6,196},{7,228},{8,12}... | collective-permute-start | bytes 786440 | tf_op jit(solution)/shard_map/ppermute | solution.py:356
  204.6 1.0 copy-start.1
  214.5 3.4 %copy-start = (f32[8192,256]{1,0:T(8,128)S(1)}, f32[8192,256]{1,0:T(8,128)}, u32[]{:S(2)}) copy-start(f32[8192,256]{1,0:T(8,128)} %copy.3) | copy-start | bytes 25165828
  217.9 1.2 copy-start.2
Sparse Core Ops, SparseCore 0:
  32.6 116.0 all-gather.2

commit v2 on v1

v2 whole, which is shorter than its diff:
```python
import functools
import jax
import jax.numpy as jnp
from jax import lax
from jax.experimental import pallas as pl
from jax.experimental.pallas import tpu as pltpu
from jax.sharding import PartitionSpec as P

B = 256
NP = 4
TOP = NP * B
F32 = jnp.float32
BF16 = jnp.bfloat16
MESH = pl.DeviceIdType.MESH


def split(a):
    hi = a.astype(BF16)
    return hi, (a - hi.astype(F32)).astype(BF16)


def dot1(a, b):
    return jnp.dot(a, b, preferred_element_type=F32)


def dot3(a, b):
    ah, al = split(a)
    bh, bl = split(b)
    return dot1(ah, bh) + (dot1(ah, bl) + dot1(al, bh))


def panel(R, j, sub, lane):
    for g in range(4):
        c0 = j + 8 * g
        lt = c0 // 128
        o = c0 % 128
        cb = {}
        for h in range(g, 4):
            for t in range(8):
                cb[h, t] = jnp.broadcast_to(R[h][lt][:, o + t:o + t + 1], (8, 128))
        inblk = (lane >= o) & (lane < o + 8)
        R[g][lt] = jnp.where(inblk, jnp.where(lane - o == sub, 1.0, 0.0), R[g][lt])
        for h in range(g + 1, 4):
            R[h][lt] = jnp.where(inblk, 0.0, R[h][lt])
        scale = jnp.zeros((8, 128), F32)
        for t in range(8):
            piv = jnp.broadcast_to(cb[g, t][t:t + 1, :], (8, 128))
            inv = 1.0 / piv
            scale = jnp.where(sub == t, lax.rsqrt(piv), scale)
            rows = [jnp.broadcast_to(R[g][l][t:t + 1, :], (8, 128)) for l in range(2)]
            crow = {u: jnp.broadcast_to(cb[g, u][t:t + 1, :], (8, 128)) for u in range(t + 1, 8)}
            for h in range(g, 4):
                f = cb[h, t] * inv
                if h == g:
                    f = jnp.where(sub > t, f, 0.0)
                for l in range(2):
                    R[h][l] = R[h][l] - f * rows[l]
                for u in range(t + 1, 8):
                    cb[h, u] = cb[h, u] - f * crow[u]
        for u in range(1, 8):
            R[g][lt] = jnp.where((lane == o + u) & (sub < u), cb[g, u], R[g][lt])
        for l in range(2):
            R[g][l] = R[g][l] * scale
    return R


def factor_tile(T, between):
    sub = lax.broadcasted_iota(jnp.int32, (8, 128), 0)
    lane = lax.broadcasted_iota(jnp.int32, (8, 128), 1)
    pr = lax.broadcasted_iota(jnp.int32, (32, B), 0)
    pc = lax.broadcasted_iota(jnp.int32, (32, B), 1)
    for jb in range(8):
        between(jb)
        j = 32 * jb
        R = [[T[j + 8 * g:j + 8 * g + 8, 128 * l:128 * l + 128] for l in range(2)] for g in range(4)]
        R = panel(R, j, sub, lane)
        rows = jnp.concatenate([jnp.concatenate(r, axis=1) for r in R], axis=0)
        T[j:j + 32, :] = rows
        if jb < 7:
            left = rows.T[j + 32:, :]
            n = B - j - 32
            ln = lax.broadcasted_iota(jnp.int32, (n, B), 1)
            low = jnp.where((ln >= j) & (ln < j + 32), 0.0, T[j + 32:, :])
            rows = jnp.where((pc < j + 32) & (pc > j + pr), 0.0, rows)
            T[j + 32:, :] = low - dot3(left, rows)


HA = 144
HB = B - HA


def main_kernel(a_ref, bulk, whi_ref, wlo_ref, l_ref,
                at, m_ref, g_ref, S, T, W,
                rg, rm, so, sf, st, rt, ss, ra, rah, rb, rbh, saz, sax, sbx, sbz):
    p = lax.axis_index("prow")
    q = lax.axis_index("pcol")
    x = q // 8
    z = q % 8
    par = p % 2
    sib = p + 1 - 2 * par

    def zat(d):
        return 8 * x + lax.rem(z + d + 16, 8)

    def xat(d):
        return lax.rem(q + 8 * d + 64, 32)

    barrier = pltpu.get_barrier_semaphore()

    def greet(pp, qq):
        pl.semaphore_signal(barrier, inc=1, device_id=(pp, qq), device_id_type=MESH)

    for d in range(1, 8):
        greet(lax.rem(p + d, 8), q)
    for d in (1, 2, 3):
        greet(p, xat(d))
    for d in (1, -1):
        greet(p, zat(d))
    from_p, from_q = z % 4, 8 * x + p
    from_self = (from_p == p) & (from_q == q)

    @pl.when(jnp.logical_not(from_self))
    def _():
        greet(from_p, from_q)

    def scatter_to(c):
        return z, 8 * x + 4 * c + p

    def scatter_self(c):
        return (z == p) & (z == 4 * c + p)

    for c in range(2):
        @pl.when((p < NP) & jnp.logical_not(scatter_self(c)))
        def _():
            greet(*scatter_to(c))
    count = 12 + jnp.where(from_self, 0, 1)
    for c in range(2):
        count = count + jnp.where((p < NP) & jnp.logical_not(scatter_self(c)), 1, 0)
    pl.semaphore_wait(barrier, count)

    def send(src, dst, ssem, rsem, pp, qq):
        return pltpu.make_async_remote_copy(
            src_ref=src, dst_ref=dst, send_sem=ssem, recv_sem=rsem,
            device_id=(pp, qq), device_id_type=MESH,
        )

    def tile(i):
        return pl.ds(pl.multiple_of(i * B, B), B)

    def gslot(k, c):
        return g_ref.at[tile(k), pl.ds(c * B, B)]

    def origin(c):
        for n, d in enumerate((2, 6, 4, None)):
            pp = sib if d is None else lax.rem(p + d, 8)
            yield send(a_ref.at[c], gslot(p, c), so.at[c, n], rg.at[p, c], pp, q)

    def relay(k, c):
        return send(gslot(k, c), gslot(k, c), sf.at[k, c], rg.at[k, c], sib, q)

    def relay_event(i, c):
        k = par + 2 * i

        @pl.when(k != p)
        def _():
            relay(k, c).wait_recv()
            relay(k, c).start()

    def tile_sends(i, kc):
        k = par + 2 * i
        d = lax.rem(z + 8 - kc, 8)
        slot = m_ref.at[tile(k), pl.ds(kc * B, B)]
        rsem = rm.at[k, kc]
        out = []
        for n, dx in enumerate((1, 3, 2)):
            out.append(((d == 0) & (x == 0), send(slot, slot, st.at[i, kc, n], rsem, p, xat(dx))))
        out.append((d < 4, send(slot, slot, st.at[i, kc, 3], rsem, p, zat(1))))
        out.append(((d == 0) | (d > 5), send(slot, slot, st.at[i, kc, 4], rsem, p, zat(-1))))
        out.append((None, send(slot, slot, st.at[i, kc, 5], rsem, sib, q)))
        return d, out

    def tile_event(i, kc):
        k = par + 2 * i

        @pl.when(k <= kc)
        def _():
            d, sends = tile_sends(i, kc)
            here = (d == 0) & (x == 0)

            @pl.when(here)
            def _():
                m_ref[tile(k), kc * B:(kc + 1) * B] = g_ref[tile(k), 0:B]

            @pl.when(jnp.logical_not(here))
            def _():
                sends[5][1].wait_recv()
            for cond, cp in sends:
                if cond is None:
                    cp.start()
                else:
                    pl.when(cond)(cp.start)

    def sibling_tile(k, kc):
        slot = m_ref.at[tile(k), pl.ds(kc * B, B)]
        return send(slot, slot, st.at[0, kc, 5], rm.at[k, kc], sib, q)

    s = 1 - 2 * par

    def scatter(c):
        pp, qq = scatter_to(c)
        return send(at.at[c], bulk.at[qq], ss.at[c], rt.at[0], pp, qq)

    def arrive():
        return send(bulk.at[q], bulk.at[q], ss.at[0], rt.at[0], from_p, from_q)

    def part(t, lo, n):
        return bulk.at[t, pl.ds(lo, n), :]

    def hop(t, lo, n, ssem, rsem, to):
        return send(part(t, lo, n), part(t, lo, n), ssem, rsem, p, to)

    def az(n, way):
        w = s * way
        t = zat(-n * w)
        return hop(t, 0, HA, saz.at[n if way > 0 else 4 + n], ra.at[t], zat(w))

    def bz(dx, n, way):
        w = s * way
        t = 8 * lax.rem(x + dx + 4, 4) + lax.rem(z - n * w + 16, 8)
        return hop(t, HA, HB, sbz.at[dx % 4, n if way > 0 else 4 + n], rb.at[t], zat(w))

    def ax(dz, way):
        t = zat(dz)
        return hop(t, 0, HA, sax.at[dz % 8, 0 if way > 0 else 1], ra.at[t], xat(way))

    def axf(dz, way):
        zz = lax.rem(z + dz + 16, 8)
        t = 8 * lax.rem(x - way + 4, 4) + zz
        h = 0 if way > 0 else 1
        return hop(t, h * (HA // 2), HA // 2, sax.at[dz % 8, 2 + h], rah.at[zz, h], xat(way))

    def bx(way):
        return hop(q, HA, HB, sbx.at[0 if way > 0 else 1], rb.at[q], xat(way))

    def bxf(way):
        h = 0 if way > 0 else 1
        return hop(xat(-way), HA + h * (HB // 2), HB // 2, sbx.at[2 + h], rbh.at[h], xat(way))

    def got(t, lo, n, rsem):
        hop(t, lo, n, saz.at[0], rsem, xat(1)).wait_recv()

    def got_a(t):
        got(t, 0, HA, ra.at[t])

    def got_b(t):
        got(t, HA, HB, rb.at[t])

    def last(way):
        return 4 if way > 0 else 3

    def start_event():
        @pl.when(from_self)
        def _():
            bulk[q] = at[0]

        @pl.when(jnp.logical_not(from_self))
        def _():
            arrive().wait_recv()
        for way in (1, -1):
            az(0, way).start()
            bx(way).start()
            bz(0, 0, way).start()
        for way in (1, -1):
            ax(0, way).start()

    def az_event(n):
        for way in (1, -1):
            if n <= last(way):
                got_a(zat(-n * s * way))
                if n < last(way):
                    az(n, way).start()
        for dz in ((n, -n) if n < 4 else (4,)):
            for way in (1, -1):
                ax(dz, way).start()

    def bx_event():
        for way in (1, -1):
            got_b(xat(-way))
            bxf(way).start()
        for dx in (1, -1):
            for way in (1, -1):
                bz(dx, 0, way).start()

    def bx2_event():
        for h in range(2):
            got(xat(2), HA + h * (HB // 2), HB // 2, rbh.at[h])
        for way in (1, -1):
            bz(2, 0, way).start()

    def bz_event(dx, n):
        for way in (1, -1):
            if n <= last(way):
                got_b(8 * lax.rem(x + dx + 4, 4) + lax.rem(z - n * s * way + 16, 8))
                if n < last(way):
                    bz(dx, n, way).start()

    def ax_event(dz):
        zz = lax.rem(z + dz + 16, 8)
        for way in (1, -1):
            got_a(8 * lax.rem(x - way + 4, 4) + zz)
            axf(dz, way).start()

    def ax2_event(dz):
        zz = lax.rem(z + dz + 16, 8)
        t = 8 * lax.rem(x + 2, 4) + zz
        for h in range(2):
            got(t, h * (HA // 2), HA // 2, rah.at[zz, h])

    E = functools.partial
    xs = (0, 1, -1, 2)
    events = {
        (0, 0): [E(tile_event, 0, 1)],
        (0, 1): [E(tile_event, 0, 2)],
        (0, 2): [E(tile_event, 0, 3)],
        (0, 3): [E(relay_event, 1, 0), bx_event],
        (0, 4): [E(az_event, 1)],
        (0, 5): [E(tile_event, 1, 2)],
        (0, 6): [E(tile_event, 1, 3)],
        (0, 7): [bx2_event],
        (1, 0): [E(az_event, 2)],
        (1, 1): [E(bz_event, 0, 1)],
        (1, 2): [E(bz_event, 1, 1)],
        (1, 3): [E(bz_event, -1, 1)],
        (1, 4): [E(az_event, 3)],
        (1, 5): [E(bz_event, 2, 1)],
        (1, 6): [E(az_event, 4)],
        (1, 7): [E(ax_event, 0)],
        (2, 0): [E(bz_event, 0, 2)],
        (2, 1): [E(bz_event, 1, 2)],
        (2, 2): [E(bz_event, -1, 2)],
        (2, 3): [E(bz_event, 2, 2)],
        (2, 4): [E(ax_event, 1), E(ax_event, -1)],
        (2, 5): [E(ax_event, 2), E(ax_event, -2)],
        (2, 6): [E(bz_event, 0, 3), E(bz_event, 1, 3)],
        (2, 7): [E(bz_event, -1, 3), E(bz_event, 2, 3)],
        (3, 0): [E(ax_event, 3), E(ax_event, -3)],
        (3, 1): [E(ax_event, 4)],
    }

    @pl.when(p < NP)
    def _():
        for cp in origin(0):
            cp.start()
        at[0] = a_ref[0].T
        at[1] = a_ref[1].T
        for c in range(2):
            pl.when(jnp.logical_not(scatter_self(c)))(scatter(c).start)
        for cp in origin(1):
            cp.start()
        for c in range(2):
            g_ref[tile(p), c * B:(c + 1) * B] = a_ref[c]
    relay_event(0, 0)
    tile_event(0, 0)
    start_event()
    S[...] = jnp.zeros_like(S)

    row = lax.broadcasted_iota(jnp.int32, (B, B), 0)
    col = lax.broadcasted_iota(jnp.int32, (B, B), 1)

    def step(k, _):
        other = lax.rem(k, 2) != par

        @pl.when(other)
        def _():
            slot = m_ref.at[tile(k), tile(k)]
            send(slot, slot, st.at[0, 0, 5], rm.at[k, k], sib, q).wait_recv()

        T[...] = S[tile(k), tile(k)] + m_ref[tile(k), tile(k)]

        def between(jb):
            for kk in range(NP):
                for ev in events.get((kk, jb), ()):
                    pl.when(k == kk)(ev)

        factor_tile(T, between)
        S[tile(k), tile(k)] = T[...]
        X = jnp.where(row >= col, T[...], 0.0)
        for kc in range(1, NP):
            pl.when(other & (k < kc))(sibling_tile(k, kc).wait_recv)

        def solve(m, _):
            S[tile(k), tile(m)] = dot3(X, S[tile(k), tile(m)] + m_ref[tile(k), tile(m)])
            return 0

        lax.fori_loop(k + 1, NP, solve, 0)

        @pl.when(k == 0)
        def _():
            relay_event(0, 1)
            relay_event(1, 1)

        for c in range(2):
            @pl.when(other)
            def _():
                relay(k, c).wait_recv()
            S[tile(k), TOP + c * B:TOP + (c + 1) * B] = dot3(
                X, S[tile(k), TOP + c * B:TOP + (c + 1) * B] + g_ref[tile(k), c * B:(c + 1) * B])

        def trail(i, _):
            left = S[tile(k), tile(i)].T

            def inner(m, _):
                S[tile(i), tile(m)] = S[tile(i), tile(m)] - dot3(left, S[tile(k), tile(m)])
                return 0

            lax.fori_loop(i, NP + 2, inner, 0)
            return 0

        lax.fori_loop(k + 1, NP, trail, 0)
        return 0

    lax.fori_loop(0, NP, step, 0)

    kq = jnp.minimum(q, NP - 1)
    kp = jnp.minimum(p, NP - 1)
    u = S[tile(kq), tile(kp)]
    u_diag = jnp.where(col > row, u, jnp.where(col == row, 1.0 / u, 0.0))
    u = jnp.where(kp == kq, u_diag, jnp.where(kq < kp, u, 0.0))
    l_ref[...] = u.T

    col2 = lax.broadcasted_iota(jnp.int32, (B, 2 * B), 1)
    row2 = lax.broadcasted_iota(jnp.int32, (B, 2 * B), 0)
    for k in (3, 2, 1, 0):
        unit = jnp.where((row2 == col2) & (q == k), 1.0, 0.0)
        acc = jnp.where((col2 < B) & (q < NP), unit, S[k * B:(k + 1) * B, TOP:TOP + 2 * B])
        for m in range(k + 1, NP):
            acc = acc - dot3(S[k * B:(k + 1) * B, m * B:(m + 1) * B], W[m * B:(m + 1) * B, :])
        X = jnp.where(row >= col, S[k * B:(k + 1) * B, k * B:(k + 1) * B], 0.0)
        w = dot3(X.T, acc)
        W[k * B:(k + 1) * B, :] = w
        hi, lo = split(w)
        whi_ref[k * B:(k + 1) * B, :] = hi
        wlo_ref[k * B:(k + 1) * B, :] = lo

    for dx in xs:
        bz_event(dx, 4)
    for dz in range(8):
        ax2_event(dz)

    @pl.when(p < NP)
    def _():
        for c in range(2):
            for cp in origin(c):
                cp.wait_send()
            pl.when(jnp.logical_not(scatter_self(c)))(scatter(c).wait_send)
    for c in range(2):
        for i in range(2):
            k = par + 2 * i
            pl.when(k != p)(relay(k, c).wait_send)
    for i in range(2):
        for kc in range(NP):
            @pl.when(par + 2 * i <= kc)
            def _():
                for cond, cp in tile_sends(i, kc)[1]:
                    if cond is None:
                        cp.wait_send()
                    else:
                        pl.when(cond)(cp.wait_send)
    for way in (1, -1):
        bx(way).wait_send()
        bxf(way).wait_send()
        for n in range(last(way)):
            az(n, way).wait_send()
            for dx in xs:
                bz(dx, n, way).wait_send()
        for dz in range(8):
            ax(dz, way).wait_send()
            axf(dz, way).wait_send()


def main(a):
    dma = pltpu.SemaphoreType.DMA
    vmem = pl.BlockSpec(memory_space=pltpu.VMEM)
    return pl.pallas_call(
        main_kernel,
        out_shape=(
            jax.ShapeDtypeStruct((32, B, B), F32),
            jax.ShapeDtypeStruct((TOP, 2 * B), BF16),
            jax.ShapeDtypeStruct((TOP, 2 * B), BF16),
            jax.ShapeDtypeStruct((B, B), F32),
        ),
        in_specs=[vmem],
        out_specs=[vmem] * 4,
        scratch_shapes=[
            pltpu.VMEM((2, B, B), F32),
            pltpu.VMEM((TOP, TOP), F32),
            pltpu.VMEM((TOP, 2 * B), F32),
            pltpu.VMEM((TOP, TOP + 2 * B), F32),
            pltpu.VMEM((B, B), F32),
            pltpu.VMEM((TOP, 2 * B), F32),
            dma((NP, 2)), dma((NP, NP)), dma((2, 4)), dma((NP, 2)), dma((2, NP, 6)),
            dma((1,)), dma((2,)), dma((32,)), dma((8, 2)), dma((32,)), dma((2,)),
            dma((7,)), dma((8, 4)), dma((4,)), dma((4, 7)),
        ],
        compiler_params=pltpu.CompilerParams(
            collective_id=1, has_side_effects=True, vmem_limit_bytes=48 * 1024 * 1024),
        cost_estimate=pl.CostEstimate(
            flops=60_000_000_000, bytes_accessed=8_000_000, transcendentals=0),
        name="main",
    )(a)


def update_kernel(b_ref, m_ref, whi_ref, wlo_ref, l_ref, o_ref):
    r = pl.program_id(0)
    p = lax.axis_index("prow")
    q = lax.axis_index("pcol")
    acc = jnp.zeros((B, 2 * B), F32)
    for k in range(NP):
        left = b_ref[k].astype(BF16)
        acc = acc + dot1(left, whi_ref[k * B:(k + 1) * B, :])
        acc = acc + dot1(left, wlo_ref[k * B:(k + 1) * B, :])
    m = m_ref[0].astype(F32)
    top = (r == 0) & (p < NP)
    factor_col = q < NP
    c0 = jnp.where(factor_col, acc[:, 0:B], m[:, 0:B] - acc[:, 0:B])
    c0 = jnp.where(top, jnp.where(factor_col, l_ref[...], 0.0), c0)
    c1 = jnp.where(top, 0.0, m[:, B:] - acc[:, B:])
    for n, part in enumerate((c0[:, :128], c0[:, 128:], c1[:, :128], c1[:, 128:])):
        o_ref[pl.ds(n, B, stride=4), :] = part


def update(bulk, mine, whi, wlo, ltile):
    return pl.pallas_call(
        update_kernel,
        grid=(8,),
        out_shape=jax.ShapeDtypeStruct((8 * 4 * B, 128), F32),
        in_specs=[
            pl.BlockSpec((4, B, B), lambda r: (2 * (r % 4) + r // 4, 0, 0)),
            pl.BlockSpec((1, B, 2 * B), lambda r: (r, 0, 0)),
            pl.BlockSpec((TOP, 2 * B), lambda r: (0, 0)),
            pl.BlockSpec((TOP, 2 * B), lambda r: (0, 0)),
            pl.BlockSpec((B, B), lambda r: (0, 0)),
        ],
        out_specs=pl.BlockSpec((4 * B, 128), lambda r: (r, 0)),
        compiler_params=pltpu.CompilerParams(vmem_limit_bytes=32 * 1024 * 1024),
        cost_estimate=pl.CostEstimate(
            flops=4_300_000_000, bytes_accessed=16_000_000, transcendentals=0),
        name="update",
    )(bulk, mine, whi, wlo, ltile)


def local(covariance):
    mine = covariance.reshape(8, B, 2, B)
    a = mine[0].astype(F32).transpose(1, 0, 2)
    mine = mine.reshape(8, B, 2 * B)
    bulk, whi, wlo, ltile = main(a)
    out = update(bulk, mine, whi, wlo, ltile)
    return out.reshape(8, 1, B, 2, 1, B)


def solution(mesh):
    in_specs = (P(None, "prow", None, None, "pcol", None),)
    out_specs = P(None, "prow", None, None, "pcol", None)
    return jax.shard_map(local, mesh=mesh, in_specs=in_specs, out_specs=out_specs, check_vma=False)
```

time: 233 us -> 193 us (0.83)
  the two profiles are of different devices: /device:TPU:245 before, /device:TPU:20 now
where the time goes in v2:
time: 193 us
  Pallas kernels  185 us (96%)
  local copies, waits for them, and re-layouts  7.66 us (4%)
    pallas_call x1, Pallas kernels, main(): pl.pallas_call(main_kernel, out_shape=(jax.ShapeDtypeStruct((32, B, B), F...  178 us
    pallas_call x1, Pallas kernels, update(): pl.pallas_call(update_kernel, grid=(8,), out_shape=jax.ShapeDtypeStruct((...  6.72 us

profile of v2, /device:TPU:20, one launch (start us, length us, event | category | flops | bytes accessed | tf_op | source)
XLA Modules:
  0.0 192.7 jit_solution(6773732187971829074)
XLA Ops:
  0.0 1.1 slice.4
  1.2 3.2 %reshape_reshape.3.m_ref = bf16[8,256,512]{2,1,0:T(8,128)(2,1)S(1)} reshape(bf16[8,1,256,2,1,256]{5,3,4,2,1,0:T(2,128)(2,1)} %param.1) | data formatting | bytes 4194304 | tf_op jit(solution)/shard_map/reshape;reshape | solution.py:555
  4.3 178.3 %main.1 = (f32[32,256,256]{2,1,0:T(8,128)}, bf16[1024,512]{1,0:T(8,128)(2,1)S(1)}, bf16[1024,512]{1,0:T(8,128)(2,1)S(1)}, f32[256,256]{1,0:T(8,128)S(1)}) custom-call(f32[2,256,256]{2,1,0:T(8,128)S(1)} %convert_bitcast_fusion.a_ref), custom_call_target="tpu_custom_call" | custom-call | flops 60000002048 | bytes 8000000 | tf_op jit(solution)/shard_map/main/pallas_call | solution.py:484
  182.6 0.0 copy-start
  182.7 3.4 %copy-done = f32[32,256,256]{2,1,0:T(8,128)S(1)} copy-done((f32[32,256,256]{2,1,0:T(8,128)S(1)}, f32[32,256,256]{2,1,0:T(8,128)}, u32[]{:S(2)}) %copy-start) | copy-done | bytes 8388632
  186.0 6.7 %update.1 = f32[8192,128]{1,0:T(8,128)} custom-call(f32[32,256,256]{2,1,0:T(8,128)S(1)} %copy-done, bf16[8,256,512]{2,1,0:T(8,128)(2,1)S(1)} %reshape_reshape.3.m_ref, bf16[1024,512]{1,0:T(8,128)(2,1)S(1)} %get-tuple-element.10.whi_ref, bf16[1024,512]{1,0:T(8,128)(2,1)S(1)} %get-tuple-element.11.wlo_ref, f32[256,256]{1,0:T(8,128)S(1)} %get-tuple-element.12.l_ref), custom_call_target="tpu_custom_call" | custom-call | flops 4300000256 | bytes 16000000 | tf_op jit(solution)/shard_map/update/pallas_call | solution.py:533
  (1 shorter events, 0.0 us)
Async XLA Ops:
  182.6 3.4 %copy-start = (f32[32,256,256]{2,1,0:T(8,128)S(1)}, f32[32,256,256]{2,1,0:T(8,128)}, u32[]{:S(2)}) copy-start(f32[32,256,256]{2,1,0:T(8,128)} %get-tuple-element.9.b_ref) | copy-start | bytes 25165828

commit v3 on v2

--- a/solution.py
+++ b/solution.py
@@ -85,13 +85,14 @@
             T[j + 32:, :] = low - dot3(left, rows)
 
 
-HA = 144
+HA = 176
 HB = B - HA
 
 
 def main_kernel(a_ref, bulk, whi_ref, wlo_ref, l_ref,
                 at, m_ref, g_ref, S, T, W,
-                rg, rm, so, sf, st, rt, ss, ra, rah, rb, rbh, saz, sax, sbx, sbz):
+                rg, so, sf, r1, r2, r3, r4, r5, s1, s2, s2b, s3, s4, s5,
+                rt, ss, ra, rah, rb, saz, sax, sbx, sbz):
     p = lax.axis_index("prow")
     q = lax.axis_index("pcol")
     x = q // 8
@@ -110,32 +111,61 @@
     def greet(pp, qq):
         pl.semaphore_signal(barrier, inc=1, device_id=(pp, qq), device_id_type=MESH)
 
+    y = p // 2
     for d in range(1, 8):
         greet(lax.rem(p + d, 8), q)
+        greet(p, zat(d))
     for d in (1, 2, 3):
         greet(p, xat(d))
-    for d in (1, -1):
-        greet(p, zat(d))
-    from_p, from_q = z % 4, 8 * x + p
-    from_self = (from_p == p) & (from_q == q)
-
-    @pl.when(jnp.logical_not(from_self))
-    def _():
-        greet(from_p, from_q)
+    count = jnp.int32(17)
+
+    from_p, from_q = lax.rem(z - p + 8, 4), 8 * x + p
+    from_self = (p == 0) & (z == 0)
 
     def scatter_to(c):
-        return z, 8 * x + 4 * c + p
+        return z, 8 * x + lax.rem(z + 4 * c + p, 8)
 
     def scatter_self(c):
-        return (z == p) & (z == 4 * c + p)
-
+        return (p == 0) & (z == 0) & (c == 0)
+
+    def greet_if(cond, pp, qq):
+        pl.when(cond)(functools.partial(greet, pp, qq))
+        return jnp.where(cond, 1, 0)
+
+    count = count + greet_if(jnp.logical_not(from_self), from_p, from_q)
     for c in range(2):
-        @pl.when((p < NP) & jnp.logical_not(scatter_self(c)))
-        def _():
-            greet(*scatter_to(c))
-    count = 12 + jnp.where(from_self, 0, 1)
-    for c in range(2):
-        count = count + jnp.where((p < NP) & jnp.logical_not(scatter_self(c)), 1, 0)
+        count = count + greet_if((p < NP) & jnp.logical_not(scatter_self(c)), *scatter_to(c))
+
+    tiles = ((0, 0, 0), (0, 1, 0), (0, 2, 1), (0, 3, 2), (1, 1, 3),
+             (1, 2, 0), (1, 3, 1), (2, 2, 2), (2, 3, 3), (3, 3, 0))
+    origin_dev = (p < NP) & (p <= q) & (q < NP)
+    plane = jnp.int32(0)
+    my_tile = jnp.int32(0)
+    for t, (k, kc, yt) in enumerate(tiles):
+        me = (p == k) & (q == kc)
+        plane = jnp.where(me, yt, plane)
+        my_tile = jnp.where(me, t, my_tile)
+        count = count + greet_if((x == 0) & (y == yt) & jnp.logical_not(me), k, kc)
+
+    def piece_targets():
+        for c in range(2):
+            for d in range(8):
+                yield c, d, (2 * plane + c), lax.rem(z + d, 8)
+
+    for c, d, pp, qq in piece_targets():
+        cond = origin_dev & jnp.logical_not((p == pp) & (q == qq))
+        count = count + greet_if(cond, pp, qq)
+    relay0 = (x == 0) & (y == 0)
+    count = count + greet_if(jnp.logical_not(relay0), par, z)
+
+    def relay_targets():
+        for dy in range(4):
+            for dx in range(4):
+                if dx or dy:
+                    yield 4 * dy + dx, 2 * lax.rem(y + dy, 4) + par, xat(dx)
+
+    for _, pp, qq in relay_targets():
+        count = count + greet_if(relay0, pp, qq)
     pl.semaphore_wait(barrier, count)
 
     def send(src, dst, ssem, rsem, pp, qq):
@@ -166,43 +196,99 @@
             relay(k, c).wait_recv()
             relay(k, c).start()
 
-    def tile_sends(i, kc):
-        k = par + 2 * i
-        d = lax.rem(z + 8 - kc, 8)
-        slot = m_ref.at[tile(k), pl.ds(kc * B, B)]
-        rsem = rm.at[k, kc]
-        out = []
-        for n, dx in enumerate((1, 3, 2)):
-            out.append(((d == 0) & (x == 0), send(slot, slot, st.at[i, kc, n], rsem, p, xat(dx))))
-        out.append((d < 4, send(slot, slot, st.at[i, kc, 3], rsem, p, zat(1))))
-        out.append(((d == 0) | (d > 5), send(slot, slot, st.at[i, kc, 4], rsem, p, zat(-1))))
-        out.append((None, send(slot, slot, st.at[i, kc, 5], rsem, sib, q)))
-        return d, out
-
-    def tile_event(i, kc):
-        k = par + 2 * i
-
-        @pl.when(k <= kc)
-        def _():
-            d, sends = tile_sends(i, kc)
-            here = (d == 0) & (x == 0)
-
-            @pl.when(here)
+    def mpart(t, lo, n):
+        k, kc, _ = tiles[t]
+        return m_ref.at[pl.ds(pl.multiple_of(k * B + lo, 16), n), pl.ds(kc * B, B)]
+
+    def one_piece(c, d, pp, qq):
+        lo = pl.multiple_of(c * 128 + 16 * qq, 16)
+        dst = m_ref.at[pl.ds(pl.multiple_of(p * B + c * 128 + 16 * qq, 16), 16), tile(q)]
+        return send(a_ref.at[0, pl.ds(lo, 16), :], dst, s1.at[c, d], r1.at[my_tile], pp, qq)
+
+    def each_piece(act):
+        for c, d, pp, qq in piece_targets():
+            cp = one_piece(c, d, pp, qq)
+            if d == 0:
+                pl.when((p != pp))(functools.partial(act, cp))
+            else:
+                act(cp)
+
+    my_lo = par * 128 + 16 * z
+
+    def my_piece(t):
+        return mpart(t, my_lo, 16)
+
+    def got_piece(t, ref, rsem):
+        send(ref, ref, s1.at[0, 0], rsem, sib, q).wait_recv()
+
+    def relay_sends(t):
+        if t == 0:
+            for n, pp, qq in relay_targets():
+                yield send(my_piece(t), my_piece(t), s2.at[n], r2.at[t], pp, qq)
+        else:
+            for n in range(3):
+                yield send(my_piece(t), my_piece(t), s2b.at[t, n], r2.at[t], p, xat(n + 1))
+
+    def relay_tile(t):
+        k, kc, yt = tiles[t]
+
+        @pl.when((x == 0) & (y == yt))
+        def _():
+            @pl.when(jnp.logical_not((p == k) & (q == kc)))
             def _():
-                m_ref[tile(k), kc * B:(kc + 1) * B] = g_ref[tile(k), 0:B]
-
-            @pl.when(jnp.logical_not(here))
+                got_piece(t, my_piece(t), r1.at[t])
+            for cp in relay_sends(t):
+                cp.start()
+
+    def in_plane(t):
+        return None if t == 0 else y == tiles[t][2]
+
+    def when(cond, f):
+        if cond is None:
+            f()
+        else:
+            pl.when(cond)(f)
+
+    def ring_send(t, d):
+        return send(my_piece(t), my_piece(t), s3.at[t, d], r3.at[t, z], p, zat(d))
+
+    def ring_tile(t):
+        def go():
+            @pl.when(jnp.logical_not((x == 0) & (y == tiles[t][2])))
             def _():
-                sends[5][1].wait_recv()
-            for cond, cp in sends:
-                if cond is None:
+                got_piece(t, my_piece(t), r2.at[t])
+            for d in (4, 3, 5, 2, 6, 1, 7):
+                ring_send(t, d).start()
+        when(in_plane(t), go)
+
+    def half_send(t, c):
+        part = mpart(t, c * 128, 128)
+        return send(part, part, s4.at[t], r4.at[t], sib, q)
+
+    def plane_sends(t):
+        part = mpart(t, par * 128, 128)
+        for n in range(3):
+            yield send(part, part, s5.at[t, n], r5.at[t], lax.rem(p + 2 * n + 2, 8), q)
+
+    def half_tile(t):
+        def go():
+            for d in range(1, 8):
+                w = lax.rem(z + d, 8)
+                got_piece(t, mpart(t, par * 128 + 16 * w, 16), r3.at[t, w])
+            if t:
+                for cp in plane_sends(t):
                     cp.start()
-                else:
-                    pl.when(cond)(cp.start)
-
-    def sibling_tile(k, kc):
-        slot = m_ref.at[tile(k), pl.ds(kc * B, B)]
-        return send(slot, slot, st.at[0, kc, 5], rm.at[k, kc], sib, q)
+            half_send(t, par).start()
+        when(in_plane(t), go)
+
+    def pass_tile(t):
+        @pl.when(y != tiles[t][2])
+        def _():
+            got_piece(t, mpart(t, par * 128, 128), r5.at[t])
+            half_send(t, par).start()
+
+    def half_got(t):
+        half_send(t, 1 - par).wait_recv()
 
     s = 1 - 2 * par
 
@@ -239,12 +325,8 @@
         h = 0 if way > 0 else 1
         return hop(t, h * (HA // 2), HA // 2, sax.at[dz % 8, 2 + h], rah.at[zz, h], xat(way))
 
-    def bx(way):
-        return hop(q, HA, HB, sbx.at[0 if way > 0 else 1], rb.at[q], xat(way))
-
-    def bxf(way):
-        h = 0 if way > 0 else 1
-        return hop(xat(-way), HA + h * (HB // 2), HB // 2, sbx.at[2 + h], rbh.at[h], xat(way))
+    def bx(n):
+        return hop(q, HA, HB, sbx.at[n], rb.at[q], xat(n + 1))
 
     def got(t, lo, n, rsem):
         hop(t, lo, n, saz.at[0], rsem, xat(1)).wait_recv()
@@ -261,14 +343,17 @@
     def start_event():
         @pl.when(from_self)
         def _():
-            bulk[q] = at[0]
+            cp = pltpu.make_async_copy(at.at[0], bulk.at[q], rt.at[0])
+            cp.start()
+            cp.wait()
 
         @pl.when(jnp.logical_not(from_self))
         def _():
             arrive().wait_recv()
+        for n in (0, 2, 1):
+            bx(n).start()
         for way in (1, -1):
             az(0, way).start()
-            bx(way).start()
             bz(0, 0, way).start()
         for way in (1, -1):
             ax(0, way).start()
@@ -284,18 +369,10 @@
                 ax(dz, way).start()
 
     def bx_event():
-        for way in (1, -1):
-            got_b(xat(-way))
-            bxf(way).start()
-        for dx in (1, -1):
+        for dx in (1, -1, 2):
+            got_b(xat(dx))
             for way in (1, -1):
                 bz(dx, 0, way).start()
-
-    def bx2_event():
-        for h in range(2):
-            got(xat(2), HA + h * (HB // 2), HB // 2, rbh.at[h])
-        for way in (1, -1):
-            bz(2, 0, way).start()
 
     def bz_event(dx, n):
         for way in (1, -1):
@@ -318,62 +395,70 @@
 
     E = functools.partial
     xs = (0, 1, -1, 2)
+    def strips_event():
+        @pl.when(p < NP)
+        def _():
+            for c in range(2):
+                for cp in origin(c):
+                    cp.start()
+                g_ref[tile(p), c * B:(c + 1) * B] = a_ref[c]
+
     events = {
-        (0, 0): [E(tile_event, 0, 1)],
-        (0, 1): [E(tile_event, 0, 2)],
-        (0, 2): [E(tile_event, 0, 3)],
-        (0, 3): [E(relay_event, 1, 0), bx_event],
-        (0, 4): [E(az_event, 1)],
-        (0, 5): [E(tile_event, 1, 2)],
-        (0, 6): [E(tile_event, 1, 3)],
-        (0, 7): [bx2_event],
-        (1, 0): [E(az_event, 2)],
-        (1, 1): [E(bz_event, 0, 1)],
-        (1, 2): [E(bz_event, 1, 1)],
-        (1, 3): [E(bz_event, -1, 1)],
+        (0, 0): [E(half_tile, t) for t in (1, 2, 3, 4)] + [E(ring_tile, t) for t in (5, 6, 7, 8)],
+        (0, 2): [start_event],
+        (0, 3): [E(half_tile, t) for t in (5, 6, 7, 8)],
+        (0, 4): [E(pass_tile, t) for t in (1, 2, 3, 4)] + [E(ring_tile, 9)],
+        (0, 5): [bx_event],
+        (0, 6): [E(az_event, 1)],
+        (0, 7): [E(pass_tile, t) for t in (5, 6, 7, 8)] + [E(half_tile, 9)],
+        (1, 0): [E(bz_event, 0, 1), strips_event],
+        (1, 1): [E(az_event, 2), E(pass_tile, 9)],
+        (1, 2): [E(bz_event, 1, 1), E(bz_event, -1, 1)],
+        (1, 3): [E(bz_event, 2, 1)],
         (1, 4): [E(az_event, 3)],
-        (1, 5): [E(bz_event, 2, 1)],
-        (1, 6): [E(az_event, 4)],
-        (1, 7): [E(ax_event, 0)],
-        (2, 0): [E(bz_event, 0, 2)],
-        (2, 1): [E(bz_event, 1, 2)],
-        (2, 2): [E(bz_event, -1, 2)],
-        (2, 3): [E(bz_event, 2, 2)],
-        (2, 4): [E(ax_event, 1), E(ax_event, -1)],
-        (2, 5): [E(ax_event, 2), E(ax_event, -2)],
-        (2, 6): [E(bz_event, 0, 3), E(bz_event, 1, 3)],
-        (2, 7): [E(bz_event, -1, 3), E(bz_event, 2, 3)],
-        (3, 0): [E(ax_event, 3), E(ax_event, -3)],
-        (3, 1): [E(ax_event, 4)],
+        (1, 5): [E(bz_event, 0, 2)],
+        (1, 6): [E(ax_event, 0), E(ax_event, 1), E(ax_event, -1)],
+        (1, 7): [E(az_event, 4), E(bz_event, 1, 2), E(bz_event, -1, 2)],
+        (2, 0): [E(bz_event, 2, 2)],
+        (2, 2): [E(bz_event, 0, 3), E(ax_event, 2), E(ax_event, -2)],
+        (2, 4): [E(bz_event, 1, 3), E(bz_event, -1, 3)],
+        (2, 6): [E(bz_event, 2, 3), E(ax_event, 3), E(ax_event, -3)],
+        (3, 0): [E(ax_event, 4)],
+        (3, 2): [E(relay_event, 0, 0), E(relay_event, 1, 0)],
+        (3, 4): [E(relay_event, 0, 1), E(relay_event, 1, 1)],
     }
 
-    @pl.when(p < NP)
-    def _():
-        for cp in origin(0):
-            cp.start()
+    def scatter_start():
         at[0] = a_ref[0].T
         at[1] = a_ref[1].T
         for c in range(2):
             pl.when(jnp.logical_not(scatter_self(c)))(scatter(c).start)
-        for cp in origin(1):
-            cp.start()
-        for c in range(2):
-            g_ref[tile(p), c * B:(c + 1) * B] = a_ref[c]
-    relay_event(0, 0)
-    tile_event(0, 0)
-    start_event()
+
+    @pl.when(origin_dev)
+    def _():
+        each_piece(lambda cp: cp.start())
+
+        @pl.when(plane == y)
+        def _():
+            lo = pl.multiple_of(my_lo, 16)
+            m_ref[pl.ds(pl.multiple_of(p * B + my_lo, 16), 16), tile(q)] = a_ref[0, pl.ds(lo, 16), :]
+    pl.when((p < NP) & (x != 0))(scatter_start)
+    for t in range(10):
+        relay_tile(t)
+    pl.when((p < NP) & (x == 0))(scatter_start)
+    ring_tile(0)
+    for t in (1, 2, 3, 4):
+        ring_tile(t)
     S[...] = jnp.zeros_like(S)
+    half_tile(0)
 
     row = lax.broadcasted_iota(jnp.int32, (B, B), 0)
     col = lax.broadcasted_iota(jnp.int32, (B, B), 1)
 
     def step(k, _):
-        other = lax.rem(k, 2) != par
-
-        @pl.when(other)
-        def _():
-            slot = m_ref.at[tile(k), tile(k)]
-            send(slot, slot, st.at[0, 0, 5], rm.at[k, k], sib, q).wait_recv()
+        for t, (kk, kc, _) in enumerate(tiles):
+            if kk == kc:
+                pl.when(k == kk)(functools.partial(half_got, t))
 
         T[...] = S[tile(k), tile(k)] + m_ref[tile(k), tile(k)]
 
@@ -385,8 +470,9 @@
         factor_tile(T, between)
         S[tile(k), tile(k)] = T[...]
         X = jnp.where(row >= col, T[...], 0.0)
-        for kc in range(1, NP):
-            pl.when(other & (k < kc))(sibling_tile(k, kc).wait_recv)
+        for t, (kk, kc, _) in enumerate(tiles):
+            if kk != kc:
+                pl.when(k == kk)(functools.partial(half_got, t))
 
         def solve(m, _):
             S[tile(k), tile(m)] = dot3(X, S[tile(k), tile(m)] + m_ref[tile(k), tile(m)])
@@ -394,18 +480,6 @@
 
         lax.fori_loop(k + 1, NP, solve, 0)
 
-        @pl.when(k == 0)
-        def _():
-            relay_event(0, 1)
-            relay_event(1, 1)
-
-        for c in range(2):
-            @pl.when(other)
-            def _():
-                relay(k, c).wait_recv()
-            S[tile(k), TOP + c * B:TOP + (c + 1) * B] = dot3(
-                X, S[tile(k), TOP + c * B:TOP + (c + 1) * B] + g_ref[tile(k), c * B:(c + 1) * B])
-
         def trail(i, _):
             left = S[tile(k), tile(i)].T
 
@@ -413,13 +487,26 @@
                 S[tile(i), tile(m)] = S[tile(i), tile(m)] - dot3(left, S[tile(k), tile(m)])
                 return 0
 
-            lax.fori_loop(i, NP + 2, inner, 0)
+            lax.fori_loop(i, NP, inner, 0)
             return 0
 
         lax.fori_loop(k + 1, NP, trail, 0)
         return 0
 
     lax.fori_loop(0, NP, step, 0)
+
+    for i in range(2):
+        for c in range(2):
+            relay(1 - par + 2 * i, c).wait_recv()
+
+    def block(i, j):
+        return S[i * B:(i + 1) * B, j * B:(j + 1) * B]
+
+    for k in range(NP):
+        acc = g_ref[k * B:(k + 1) * B, :]
+        for i in range(k):
+            acc = acc - dot3(block(i, k).T, W[i * B:(i + 1) * B, :])
+        W[k * B:(k + 1) * B, :] = dot3(jnp.where(row >= col, block(k, k), 0.0), acc)
 
     kq = jnp.minimum(q, NP - 1)
     kp = jnp.minimum(p, NP - 1)
@@ -432,7 +519,7 @@
     row2 = lax.broadcasted_iota(jnp.int32, (B, 2 * B), 0)
     for k in (3, 2, 1, 0):
         unit = jnp.where((row2 == col2) & (q == k), 1.0, 0.0)
-        acc = jnp.where((col2 < B) & (q < NP), unit, S[k * B:(k + 1) * B, TOP:TOP + 2 * B])
+        acc = jnp.where((col2 < B) & (q < NP), unit, W[k * B:(k + 1) * B, :])
         for m in range(k + 1, NP):
             acc = acc - dot3(S[k * B:(k + 1) * B, m * B:(m + 1) * B], W[m * B:(m + 1) * B, :])
         X = jnp.where(row >= col, S[k * B:(k + 1) * B, k * B:(k + 1) * B], 0.0)
@@ -457,18 +544,24 @@
         for i in range(2):
             k = par + 2 * i
             pl.when(k != p)(relay(k, c).wait_send)
-    for i in range(2):
-        for kc in range(NP):
-            @pl.when(par + 2 * i <= kc)
-            def _():
-                for cond, cp in tile_sends(i, kc)[1]:
-                    if cond is None:
-                        cp.wait_send()
-                    else:
-                        pl.when(cond)(cp.wait_send)
+    pl.when(origin_dev)(lambda: each_piece(lambda cp: cp.wait_send()))
+    for t in range(10):
+        @pl.when((x == 0) & (y == tiles[t][2]))
+        def _():
+            for cp in relay_sends(t):
+                cp.wait_send()
+
+        def drain():
+            for d in range(1, 8):
+                ring_send(t, d).wait_send()
+            if t:
+                for cp in plane_sends(t):
+                    cp.wait_send()
+        when(in_plane(t), drain)
+        half_send(t, par).wait_send()
+    for n in range(3):
+        bx(n).wait_send()
     for way in (1, -1):
-        bx(way).wait_send()
-        bxf(way).wait_send()
         for n in range(last(way)):
             az(n, way).wait_send()
             for dx in xs:
@@ -495,28 +588,30 @@
             pltpu.VMEM((2, B, B), F32),
             pltpu.VMEM((TOP, TOP), F32),
             pltpu.VMEM((TOP, 2 * B), F32),
-            pltpu.VMEM((TOP, TOP + 2 * B), F32),
+            pltpu.VMEM((TOP, TOP), F32),
             pltpu.VMEM((B, B), F32),
             pltpu.VMEM((TOP, 2 * B), F32),
-            dma((NP, 2)), dma((NP, NP)), dma((2, 4)), dma((NP, 2)), dma((2, NP, 6)),
-            dma((1,)), dma((2,)), dma((32,)), dma((8, 2)), dma((32,)), dma((2,)),
-            dma((7,)), dma((8, 4)), dma((4,)), dma((4, 7)),
+            dma((NP, 2)), dma((2, 4)), dma((NP, 2)),
+            dma((10,)), dma((10,)), dma((10, 8)), dma((10,)), dma((10,)),
+            dma((2, 8)), dma((16,)), dma((10, 3)), dma((10, 8)), dma((10,)), dma((10, 3)),
+            dma((1,)), dma((2,)), dma((32,)), dma((8, 2)), dma((32,)),
+            dma((7,)), dma((8, 4)), dma((3,)), dma((4, 7)),
         ],
         compiler_params=pltpu.CompilerParams(
-            collective_id=1, has_side_effects=True, vmem_limit_bytes=48 * 1024 * 1024),
+            collective_id=1, has_side_effects=True, vmem_limit_bytes=30 * 1024 * 1024),
         cost_estimate=pl.CostEstimate(
             flops=60_000_000_000, bytes_accessed=8_000_000, transcendentals=0),
         name="main",
     )(a)
 
 
-def update_kernel(b_ref, m_ref, whi_ref, wlo_ref, l_ref, o_ref):
+def update_kernel(p_ref, b0, b1, b2, b3, m_ref, whi_ref, wlo_ref, l_ref, o_ref):
     r = pl.program_id(0)
-    p = lax.axis_index("prow")
-    q = lax.axis_index("pcol")
+    p = p_ref[0]
+    q = p_ref[1]
     acc = jnp.zeros((B, 2 * B), F32)
-    for k in range(NP):
-        left = b_ref[k].astype(BF16)
+    for k, b_ref in enumerate((b0, b1, b2, b3)):
+        left = b_ref[0].astype(BF16)
         acc = acc + dot1(left, whi_ref[k * B:(k + 1) * B, :])
         acc = acc + dot1(left, wlo_ref[k * B:(k + 1) * B, :])
     m = m_ref[0].astype(F32)
@@ -529,24 +624,31 @@
         o_ref[pl.ds(n, B, stride=4), :] = part
 
 
-def update(bulk, mine, whi, wlo, ltile):
+def update(place, bulk, mine, whi, wlo, ltile):
+    def stream(k):
+        def index(r, place):
+            return 8 * (r % 4) + (place[0] + 4 * (r // 4) + k) % 8, 0, 0
+        return pl.BlockSpec((1, B, B), index)
+
     return pl.pallas_call(
         update_kernel,
-        grid=(8,),
         out_shape=jax.ShapeDtypeStruct((8 * 4 * B, 128), F32),
-        in_specs=[
-            pl.BlockSpec((4, B, B), lambda r: (2 * (r % 4) + r // 4, 0, 0)),
-            pl.BlockSpec((1, B, 2 * B), lambda r: (r, 0, 0)),
-            pl.BlockSpec((TOP, 2 * B), lambda r: (0, 0)),
-            pl.BlockSpec((TOP, 2 * B), lambda r: (0, 0)),
-            pl.BlockSpec((B, B), lambda r: (0, 0)),
-        ],
-        out_specs=pl.BlockSpec((4 * B, 128), lambda r: (r, 0)),
-        compiler_params=pltpu.CompilerParams(vmem_limit_bytes=32 * 1024 * 1024),
+        grid_spec=pltpu.PrefetchScalarGridSpec(
+            num_scalar_prefetch=1,
+            grid=(8,),
+            in_specs=[stream(k) for k in range(NP)] + [
+                pl.BlockSpec((1, B, 2 * B), lambda r, place: (r, 0, 0)),
+                pl.BlockSpec((TOP, 2 * B), lambda r, place: (0, 0)),
+                pl.BlockSpec((TOP, 2 * B), lambda r, place: (0, 0)),
+                pl.BlockSpec((B, B), lambda r, place: (0, 0)),
+            ],
+            out_specs=pl.BlockSpec((4 * B, 128), lambda r, place: (r, 0)),
+        ),
+        compiler_params=pltpu.CompilerParams(vmem_limit_bytes=20 * 1024 * 1024),
         cost_estimate=pl.CostEstimate(
             flops=4_300_000_000, bytes_accessed=16_000_000, transcendentals=0),
         name="update",
-    )(bulk, mine, whi, wlo, ltile)
+    )(place, bulk, bulk, bulk, bulk, mine, whi, wlo, ltile)
 
 
 def local(covariance):
@@ -554,7 +656,8 @@
     a = mine[0].astype(F32).transpose(1, 0, 2)
     mine = mine.reshape(8, B, 2 * B)
     bulk, whi, wlo, ltile = main(a)
-    out = update(bulk, mine, whi, wlo, ltile)
+    place = jnp.stack([lax.axis_index("prow"), lax.axis_index("pcol")]).astype(jnp.int32)
+    out = update(place, bulk, mine, whi, wlo, ltile)
     return out.reshape(8, 1, B, 2, 1, B)
 
 

time: 193 us -> 120 us (0.62)
  the two profiles are of different devices: /device:TPU:20 before, /device:TPU:2 now
where the time goes in v3:
time: 120 us; the launch traced here: 119 us
  Pallas kernels  115 us (96%)
  local copies, waits for them, and re-layouts  4.29 us (4%)
    pallas_call x1, Pallas kernels, main(): pl.pallas_call(main_kernel, out_shape=(jax.ShapeDtypeStruct((32, B, B), F...  108 us
    pallas_call x1, Pallas kernels, update(): pl.pallas_call(update_kernel, out_shape=jax.ShapeDtypeStruct((8 * 4 * B,...  7.29 us
    another operation x1, local copies, waits for them, and re-layouts, local(): mine = mine.reshape(8, B, 2 * B)  3.16 us

profile of v3, /device:TPU:2, one launch (start us, length us, event | category | flops | bytes accessed | tf_op | source)
XLA Modules:
  0.0 119.5 jit_solution(17952859909721055354)
XLA Ops:
  0.0 0.1 pad_add_fusion.p_ref
  0.1 1.1 slice.4
  1.3 3.2 %reshape_reshape.3.m_ref = bf16[8,256,512]{2,1,0:T(8,128)(2,1)S(1)} reshape(bf16[8,1,256,2,1,256]{5,3,4,2,1,0:T(2,128)(2,1)} %param.1) | data formatting | bytes 4194304 | tf_op jit(solution)/shard_map/reshape;reshape | solution.py:657
  4.4 107.7 %main.1 = (f32[32,256,256]{2,1,0:T(8,128)S(1)}, bf16[1024,512]{1,0:T(8,128)(2,1)S(1)}, bf16[1024,512]{1,0:T(8,128)(2,1)S(1)}, f32[256,256]{1,0:T(8,128)S(1)}) custom-call(f32[2,256,256]{2,1,0:T(8,128)S(1)} %convert_bitcast_fusion.a_ref), custom_call_target="tpu_custom_call" | custom-call | flops 60000002048 | bytes 8000000 | tf_op jit(solution)/shard_map/main/pallas_call | solution.py:577
  112.2 7.3 %update.1 = f32[8192,128]{1,0:T(8,128)} custom-call(s32[2]{0:T(128)S(1)} %pad_add_fusion.p_ref, f32[32,256,256]{2,1,0:T(8,128)S(1)} %get-tuple-element.9.b0.b1.b2.b3, f32[32,256,256]{2,1,0:T(8,128)S(1)} %get-tuple-element.9.b0.b1.b2.b3, f32[32,256,256]{2,1,0:T(8,128)S(1)} %get-tuple-element.9.b0.b1.b2.b3, f32[32,256,256]{2,1,0:T(8,128)S(1)} %get-tuple-element.9.b0.b1.b2.b3, ...), custom_call_target="tpu_custom_call" | custom-call | flops 4300000256 | bytes 16000000 | tf_op jit(solution)/shard_map/update/pallas_call | solution.py:633
  (1 shorter events, 0.0 us)

commit v4 on v3

--- a/solution.py
+++ b/solution.py
@@ -85,13 +85,13 @@
             T[j + 32:, :] = low - dot3(left, rows)
 
 
-HA = 176
+HA = 160
 HB = B - HA
 
 
 def main_kernel(a_ref, bulk, whi_ref, wlo_ref, l_ref,
                 at, m_ref, g_ref, S, T, W,
-                rg, so, sf, r1, r2, r3, r4, r5, s1, s2, s2b, s3, s4, s5,
+                rg, so, sf, sg, r1, r2, r3, r4, r5, s1, s2, s2b, s3, s4, s5,
                 rt, ss, ra, rah, rb, saz, sax, sbx, sbz):
     p = lax.axis_index("prow")
     q = lax.axis_index("pcol")
@@ -181,20 +181,30 @@
         return g_ref.at[tile(k), pl.ds(c * B, B)]
 
     def origin(c):
-        for n, d in enumerate((2, 6, 4, None)):
+        for n, d in enumerate((2, 6, None)):
             pp = sib if d is None else lax.rem(p + d, 8)
             yield send(a_ref.at[c], gslot(p, c), so.at[c, n], rg.at[p, c], pp, q)
 
     def relay(k, c):
         return send(gslot(k, c), gslot(k, c), sf.at[k, c], rg.at[k, c], sib, q)
 
-    def relay_event(i, c):
+    def onward(i, c):
         k = par + 2 * i
-
-        @pl.when(k != p)
+        pp = lax.rem(p + (2 if c == 0 else 6), 8)
+        return y == (i + (1 if c == 0 else 3)) % 4, send(
+            gslot(k, c), gslot(k, c), sg.at[i, c], rg.at[k, c], pp, q)
+
+    def relay_event(i, c, far):
+        k = par + 2 * i
+        opposite = y == (i + 2) % 4
+
+        @pl.when(opposite if far else (k != p) & jnp.logical_not(opposite))
         def _():
             relay(k, c).wait_recv()
             relay(k, c).start()
+            if not far:
+                cond, cp = onward(i, c)
+                pl.when(cond)(cp.start)
 
     def mpart(t, lo, n):
         k, kc, _ = tiles[t]
@@ -404,28 +414,27 @@
                 g_ref[tile(p), c * B:(c + 1) * B] = a_ref[c]
 
     events = {
-        (0, 0): [E(half_tile, t) for t in (1, 2, 3, 4)] + [E(ring_tile, t) for t in (5, 6, 7, 8)],
-        (0, 2): [start_event],
-        (0, 3): [E(half_tile, t) for t in (5, 6, 7, 8)],
-        (0, 4): [E(pass_tile, t) for t in (1, 2, 3, 4)] + [E(ring_tile, 9)],
-        (0, 5): [bx_event],
-        (0, 6): [E(az_event, 1)],
-        (0, 7): [E(pass_tile, t) for t in (5, 6, 7, 8)] + [E(half_tile, 9)],
-        (1, 0): [E(bz_event, 0, 1), strips_event],
-        (1, 1): [E(az_event, 2), E(pass_tile, 9)],
-        (1, 2): [E(bz_event, 1, 1), E(bz_event, -1, 1)],
-        (1, 3): [E(bz_event, 2, 1)],
-        (1, 4): [E(az_event, 3)],
+        (0, 0): [E(half_tile, t) for t in (1, 2, 3, 4)],
+        (0, 1): [start_event],
+        (0, 2): [E(half_tile, t) for t in (5, 6, 7, 8, 9)],
+        (0, 5): [E(pass_tile, t) for t in (1, 2, 3, 4)],
+        (0, 6): [E(az_event, 1), strips_event],
+        (0, 7): [bx_event, E(bz_event, 0, 1)],
+        (1, 0): [E(pass_tile, t) for t in (5, 6, 7, 8, 9)] + [E(ax_event, 0)],
+        (1, 3): [E(az_event, 2)],
+        (1, 4): [E(bz_event, dx, 1) for dx in (1, -1, 2)],
         (1, 5): [E(bz_event, 0, 2)],
-        (1, 6): [E(ax_event, 0), E(ax_event, 1), E(ax_event, -1)],
-        (1, 7): [E(az_event, 4), E(bz_event, 1, 2), E(bz_event, -1, 2)],
-        (2, 0): [E(bz_event, 2, 2)],
-        (2, 2): [E(bz_event, 0, 3), E(ax_event, 2), E(ax_event, -2)],
-        (2, 4): [E(bz_event, 1, 3), E(bz_event, -1, 3)],
-        (2, 6): [E(bz_event, 2, 3), E(ax_event, 3), E(ax_event, -3)],
-        (3, 0): [E(ax_event, 4)],
-        (3, 2): [E(relay_event, 0, 0), E(relay_event, 1, 0)],
-        (3, 4): [E(relay_event, 0, 1), E(relay_event, 1, 1)],
+        (1, 6): [E(ax_event, 1), E(ax_event, -1)],
+        (1, 7): [E(relay_event, i, c, False) for c in range(2) for i in range(2)],
+        (2, 0): [E(az_event, 3)],
+        (2, 1): [E(bz_event, dx, 2) for dx in (1, -1, 2)],
+        (2, 2): [E(ax_event, 2), E(ax_event, -2)],
+        (2, 3): [E(bz_event, 0, 3)],
+        (2, 5): [E(relay_event, i, c, True) for c in range(2) for i in range(2)],
+        (2, 7): [E(az_event, 4)],
+        (3, 0): [E(bz_event, dx, 3) for dx in (1, -1, 2)],
+        (3, 1): [E(ax_event, 3), E(ax_event, -3)],
+        (3, 6): [E(ax_event, 4)],
     }
 
     def scatter_start():
@@ -443,11 +452,12 @@
             lo = pl.multiple_of(my_lo, 16)
             m_ref[pl.ds(pl.multiple_of(p * B + my_lo, 16), 16), tile(q)] = a_ref[0, pl.ds(lo, 16), :]
     pl.when((p < NP) & (x != 0))(scatter_start)
-    for t in range(10):
+    relay_tile(0)
+    pl.when((p < NP) & (x == 0))(scatter_start)
+    for t in range(1, 10):
         relay_tile(t)
-    pl.when((p < NP) & (x == 0))(scatter_start)
     ring_tile(0)
-    for t in (1, 2, 3, 4):
+    for t in range(1, 10):
         ring_tile(t)
     S[...] = jnp.zeros_like(S)
     half_tile(0)
@@ -544,6 +554,8 @@
         for i in range(2):
             k = par + 2 * i
             pl.when(k != p)(relay(k, c).wait_send)
+            cond, cp = onward(i, c)
+            pl.when(cond)(cp.wait_send)
     pl.when(origin_dev)(lambda: each_piece(lambda cp: cp.wait_send()))
     for t in range(10):
         @pl.when((x == 0) & (y == tiles[t][2]))
@@ -591,7 +603,7 @@
             pltpu.VMEM((TOP, TOP), F32),
             pltpu.VMEM((B, B), F32),
             pltpu.VMEM((TOP, 2 * B), F32),
-            dma((NP, 2)), dma((2, 4)), dma((NP, 2)),
+            dma((NP, 2)), dma((2, 3)), dma((NP, 2)), dma((2, 2)),
             dma((10,)), dma((10,)), dma((10, 8)), dma((10,)), dma((10,)),
             dma((2, 8)), dma((16,)), dma((10, 3)), dma((10, 8)), dma((10,)), dma((10, 3)),
             dma((1,)), dma((2,)), dma((32,)), dma((8, 2)), dma((32,)),

time: 120 us -> 113 us (0.942)
  the two profiles are of different devices: /device:TPU:2 before, /device:TPU:9 now
where the time goes in v4:
time: 113 us; the launch traced here: 111 us
  Pallas kernels  107 us (95%)
  local copies, waits for them, and re-layouts  4.29 us (4%)
    pallas_call x1, Pallas kernels, main(): pl.pallas_call(main_kernel, out_shape=(jax.ShapeDtypeStruct((32, B, B), F...  99.4 us
    pallas_call x1, Pallas kernels, update(): pl.pallas_call(update_kernel, out_shape=jax.ShapeDtypeStruct((8 * 4 * B,...  7.29 us
    another operation x1, local copies, waits for them, and re-layouts, local(): mine = mine.reshape(8, B, 2 * B)  3.16 us

profile of v4, /device:TPU:9, one launch (start us, length us, event | category | flops | bytes accessed | tf_op | source)
XLA Modules:
  0.0 111.1 jit_solution(7207877065082121967)
XLA Ops:
  0.0 0.1 pad_add_fusion.p_ref
  0.1 1.1 %slice.4 = bf16[1,1,256,2,1,256]{5,3,4,2,1,0:T(2,128)(2,1)S(1)} slice(bf16[8,1,256,2,1,256]{5,3,4,2,1,0:T(2,128)(2,1)} %param.1), slice={[0:1], [0:1], [0:256], [0:2], [0:1], [0:256]} | slice | bytes 524288 | tf_op jit(solution)/shard_map/slice | solution.py:668
  1.3 3.2 %reshape_reshape.3.m_ref = bf16[8,256,512]{2,1,0:T(8,128)(2,1)S(1)} reshape(bf16[8,1,256,2,1,256]{5,3,4,2,1,0:T(2,128)(2,1)} %param.1) | data formatting | bytes 4194304 | tf_op jit(solution)/shard_map/reshape;reshape | solution.py:669
  4.4 99.4 %main.1 = (f32[32,256,256]{2,1,0:T(8,128)S(1)}, bf16[1024,512]{1,0:T(8,128)(2,1)S(1)}, bf16[1024,512]{1,0:T(8,128)(2,1)S(1)}, f32[256,256]{1,0:T(8,128)S(1)}) custom-call(f32[2,256,256]{2,1,0:T(8,128)S(1)} %convert_bitcast_fusion.a_ref), custom_call_target="tpu_custom_call" | custom-call | flops 60000002048 | bytes 8000000 | tf_op jit(solution)/shard_map/main/pallas_call | solution.py:589
  103.8 7.3 %update.1 = f32[8192,128]{1,0:T(8,128)} custom-call(s32[2]{0:T(128)S(1)} %pad_add_fusion.p_ref, f32[32,256,256]{2,1,0:T(8,128)S(1)} %get-tuple-element.9.b0.b1.b2.b3, f32[32,256,256]{2,1,0:T(8,128)S(1)} %get-tuple-element.9.b0.b1.b2.b3, f32[32,256,256]{2,1,0:T(8,128)S(1)} %get-tuple-element.9.b0.b1.b2.b3, f32[32,256,256]{2,1,0:T(8,128)S(1)} %get-tuple-element.9.b0.b1.b2.b3, ...), custom_call_target="tpu_custom_call" | custom-call | flops 4300000256 | bytes 16000000 | tf_op jit(solution)/shard_map/update/pallas_call | solution.py:645
  (1 shorter events, 0.0 us)

commit v5 on v4

--- a/solution.py
+++ b/solution.py
@@ -92,7 +92,7 @@
 def main_kernel(a_ref, bulk, whi_ref, wlo_ref, l_ref,
                 at, m_ref, g_ref, S, T, W,
                 rg, so, sf, sg, r1, r2, r3, r4, r5, s1, s2, s2b, s3, s4, s5,
-                rt, ss, ra, rah, rb, saz, sax, sbx, sbz):
+                rt, ss, ra, rah, rb, rbx, saz, sax, sbx, sbz):
     p = lax.axis_index("prow")
     q = lax.axis_index("pcol")
     x = q // 8
@@ -302,76 +302,92 @@
 
     s = 1 - 2 * par
 
-    def scatter(c):
+    def xm(d):
+        return lax.rem(x + d + 4, 4)
+
+    def zm(d):
+        return lax.rem(z + d + 16, 8)
+
+    def scatter(c, b):
         pp, qq = scatter_to(c)
-        return send(at.at[c], bulk.at[qq], ss.at[c], rt.at[0], pp, qq)
-
-    def arrive():
-        return send(bulk.at[q], bulk.at[q], ss.at[0], rt.at[0], from_p, from_q)
-
-    def part(t, lo, n):
-        return bulk.at[t, pl.ds(lo, n), :]
-
-    def hop(t, lo, n, ssem, rsem, to):
-        return send(part(t, lo, n), part(t, lo, n), ssem, rsem, p, to)
+        rows = pl.ds(HA, HB) if b else pl.ds(0, HA)
+        return send(at.at[c, rows, :], bulk.at[lax.rem(z + 4 * c + p, 8), x, rows, :],
+                    ss.at[c, b], rt.at[b], pp, qq)
+
+    def hop(ref, ssem, rsem, to):
+        return send(ref, ref, ssem, rsem, p, to)
+
+    def got(ref, rsem):
+        hop(ref, saz.at[0], rsem, xat(1)).wait_recv()
+
+    def part_a(zz, xx):
+        return bulk.at[zz, xx, pl.ds(0, HA), :]
+
+    def half_a(zz, xx, h):
+        return bulk.at[zz, xx, pl.ds(h * (HA // 2), HA // 2), :]
+
+    def part_b(zz, xx):
+        return bulk.at[zz, xx, pl.ds(HA, HB), :]
+
+    def row_b(zz):
+        return bulk.at[zz, :, pl.ds(HA, HB), :]
 
     def az(n, way):
         w = s * way
-        t = zat(-n * w)
-        return hop(t, 0, HA, saz.at[n if way > 0 else 4 + n], ra.at[t], zat(w))
-
-    def bz(dx, n, way):
+        zz = zm(-n * w)
+        return hop(part_a(zz, x), saz.at[n if way > 0 else 4 + n], ra.at[zz, x], zat(w))
+
+    def bz(n, way):
         w = s * way
-        t = 8 * lax.rem(x + dx + 4, 4) + lax.rem(z - n * w + 16, 8)
-        return hop(t, HA, HB, sbz.at[dx % 4, n if way > 0 else 4 + n], rb.at[t], zat(w))
+        zz = zm(-n * w)
+        return hop(row_b(zz), sbz.at[n if way > 0 else 4 + n], rb.at[zz], zat(w))
 
     def ax(dz, way):
-        t = zat(dz)
-        return hop(t, 0, HA, sax.at[dz % 8, 0 if way > 0 else 1], ra.at[t], xat(way))
+        zz = zm(dz)
+        return hop(part_a(zz, x), sax.at[dz % 8, 0 if way > 0 else 1], ra.at[zz, x], xat(way))
 
     def axf(dz, way):
-        zz = lax.rem(z + dz + 16, 8)
-        t = 8 * lax.rem(x - way + 4, 4) + zz
+        zz = zm(dz)
         h = 0 if way > 0 else 1
-        return hop(t, h * (HA // 2), HA // 2, sax.at[dz % 8, 2 + h], rah.at[zz, h], xat(way))
+        return hop(half_a(zz, xm(-way), h), sax.at[dz % 8, 2 + h], rah.at[zz, h], xat(way))
 
     def bx(n):
-        return hop(q, HA, HB, sbx.at[n], rb.at[q], xat(n + 1))
-
-    def got(t, lo, n, rsem):
-        hop(t, lo, n, saz.at[0], rsem, xat(1)).wait_recv()
-
-    def got_a(t):
-        got(t, 0, HA, ra.at[t])
-
-    def got_b(t):
-        got(t, HA, HB, rb.at[t])
+        return hop(part_b(z, x), sbx.at[n], rbx.at[x], xat(n + 1))
 
     def last(way):
         return 4 if way > 0 else 3
 
-    def start_event():
+    def arrive(b):
+        rows = pl.ds(HA, HB) if b else pl.ds(0, HA)
+        own = bulk.at[z, x, rows, :]
+
         @pl.when(from_self)
         def _():
-            cp = pltpu.make_async_copy(at.at[0], bulk.at[q], rt.at[0])
+            cp = pltpu.make_async_copy(at.at[0, rows, :], own, rt.at[b])
             cp.start()
             cp.wait()
 
         @pl.when(jnp.logical_not(from_self))
         def _():
-            arrive().wait_recv()
+            send(own, own, ss.at[0, b], rt.at[b], from_p, from_q).wait_recv()
+
+    def start_b_event():
+        arrive(1)
         for n in (0, 2, 1):
             bx(n).start()
+
+    def start_event():
+        arrive(0)
         for way in (1, -1):
             az(0, way).start()
-            bz(0, 0, way).start()
         for way in (1, -1):
             ax(0, way).start()
 
     def az_event(n):
         for way in (1, -1):
             if n <= last(way):
-                got_a(zat(-n * s * way))
+                zz = zm(-n * s * way)
+                got(part_a(zz, x), ra.at[zz, x])
                 if n < last(way):
                     az(n, way).start()
         for dz in ((n, -n) if n < 4 else (4,)):
@@ -380,31 +396,30 @@
 
     def bx_event():
         for dx in (1, -1, 2):
-            got_b(xat(dx))
-            for way in (1, -1):
-                bz(dx, 0, way).start()
-
-    def bz_event(dx, n):
+            got(part_b(z, xm(dx)), rbx.at[xm(dx)])
+        for way in (1, -1):
+            bz(0, way).start()
+
+    def bz_event(n):
         for way in (1, -1):
             if n <= last(way):
-                got_b(8 * lax.rem(x + dx + 4, 4) + lax.rem(z - n * s * way + 16, 8))
+                zz = zm(-n * s * way)
+                got(row_b(zz), rb.at[zz])
                 if n < last(way):
-                    bz(dx, n, way).start()
+                    bz(n, way).start()
 
     def ax_event(dz):
-        zz = lax.rem(z + dz + 16, 8)
+        zz = zm(dz)
         for way in (1, -1):
-            got_a(8 * lax.rem(x - way + 4, 4) + zz)
+            got(part_a(zz, xm(-way)), ra.at[zz, xm(-way)])
             axf(dz, way).start()
 
     def ax2_event(dz):
-        zz = lax.rem(z + dz + 16, 8)
-        t = 8 * lax.rem(x + 2, 4) + zz
+        zz = zm(dz)
         for h in range(2):
-            got(t, h * (HA // 2), HA // 2, rah.at[zz, h])
+            got(half_a(zz, xm(2), h), rah.at[zz, h])
 
     E = functools.partial
-    xs = (0, 1, -1, 2)
     def strips_event():
         @pl.when(p < NP)
         def _():
@@ -415,33 +430,30 @@
 
     events = {
         (0, 0): [E(half_tile, t) for t in (1, 2, 3, 4)],
-        (0, 1): [start_event],
         (0, 2): [E(half_tile, t) for t in (5, 6, 7, 8, 9)],
         (0, 5): [E(pass_tile, t) for t in (1, 2, 3, 4)],
-        (0, 6): [E(az_event, 1), strips_event],
-        (0, 7): [bx_event, E(bz_event, 0, 1)],
-        (1, 0): [E(pass_tile, t) for t in (5, 6, 7, 8, 9)] + [E(ax_event, 0)],
-        (1, 3): [E(az_event, 2)],
-        (1, 4): [E(bz_event, dx, 1) for dx in (1, -1, 2)],
-        (1, 5): [E(bz_event, 0, 2)],
-        (1, 6): [E(ax_event, 1), E(ax_event, -1)],
+        (0, 6): [strips_event],
+        (0, 7): [E(az_event, 1)],
+        (1, 0): [E(pass_tile, t) for t in (5, 6, 7, 8, 9)] + [E(bz_event, 1)],
+        (1, 4): [E(ax_event, 0)],
+        (1, 5): [E(az_event, 2)],
         (1, 7): [E(relay_event, i, c, False) for c in range(2) for i in range(2)],
-        (2, 0): [E(az_event, 3)],
-        (2, 1): [E(bz_event, dx, 2) for dx in (1, -1, 2)],
-        (2, 2): [E(ax_event, 2), E(ax_event, -2)],
-        (2, 3): [E(bz_event, 0, 3)],
+        (2, 0): [E(bz_event, 2), E(ax_event, 1), E(ax_event, -1)],
+        (2, 3): [E(az_event, 3)],
         (2, 5): [E(relay_event, i, c, True) for c in range(2) for i in range(2)],
-        (2, 7): [E(az_event, 4)],
-        (3, 0): [E(bz_event, dx, 3) for dx in (1, -1, 2)],
-        (3, 1): [E(ax_event, 3), E(ax_event, -3)],
-        (3, 6): [E(ax_event, 4)],
+        (2, 6): [E(ax_event, 2), E(ax_event, -2)],
+        (3, 0): [E(bz_event, 3)],
+        (3, 1): [E(az_event, 4)],
+        (3, 3): [E(ax_event, 3), E(ax_event, -3)],
+        (3, 7): [E(ax_event, 4)],
     }
 
     def scatter_start():
         at[0] = a_ref[0].T
         at[1] = a_ref[1].T
-        for c in range(2):
-            pl.when(jnp.logical_not(scatter_self(c)))(scatter(c).start)
+        for b in (1, 0):
+            for c in range(2):
+                pl.when(jnp.logical_not(scatter_self(c)))(scatter(c, b).start)
 
     @pl.when(origin_dev)
     def _():
@@ -451,16 +463,18 @@
         def _():
             lo = pl.multiple_of(my_lo, 16)
             m_ref[pl.ds(pl.multiple_of(p * B + my_lo, 16), 16), tile(q)] = a_ref[0, pl.ds(lo, 16), :]
-    pl.when((p < NP) & (x != 0))(scatter_start)
+    pl.when(p < NP)(scatter_start)
     relay_tile(0)
-    pl.when((p < NP) & (x == 0))(scatter_start)
+    ring_tile(0)
     for t in range(1, 10):
         relay_tile(t)
-    ring_tile(0)
+    S[...] = jnp.zeros_like(S)
+    start_b_event()
+    half_tile(0)
     for t in range(1, 10):
         ring_tile(t)
-    S[...] = jnp.zeros_like(S)
-    half_tile(0)
+    start_event()
+    bx_event()
 
     row = lax.broadcasted_iota(jnp.int32, (B, B), 0)
     col = lax.broadcasted_iota(jnp.int32, (B, B), 1)
@@ -539,8 +553,7 @@
         whi_ref[k * B:(k + 1) * B, :] = hi
         wlo_ref[k * B:(k + 1) * B, :] = lo
 
-    for dx in xs:
-        bz_event(dx, 4)
+    bz_event(4)
     for dz in range(8):
         ax2_event(dz)
 
@@ -549,7 +562,8 @@
         for c in range(2):
             for cp in origin(c):
                 cp.wait_send()
-            pl.when(jnp.logical_not(scatter_self(c)))(scatter(c).wait_send)
+            for b in (1, 0):
+                pl.when(jnp.logical_not(scatter_self(c)))(scatter(c, b).wait_send)
     for c in range(2):
         for i in range(2):
             k = par + 2 * i
@@ -576,8 +590,7 @@
     for way in (1, -1):
         for n in range(last(way)):
             az(n, way).wait_send()
-            for dx in xs:
-                bz(dx, n, way).wait_send()
+            bz(n, way).wait_send()
         for dz in range(8):
             ax(dz, way).wait_send()
             axf(dz, way).wait_send()
@@ -589,7 +602,7 @@
     return pl.pallas_call(
         main_kernel,
         out_shape=(
-            jax.ShapeDtypeStruct((32, B, B), F32),
+            jax.ShapeDtypeStruct((8, 4, B, B), F32),
             jax.ShapeDtypeStruct((TOP, 2 * B), BF16),
             jax.ShapeDtypeStruct((TOP, 2 * B), BF16),
             jax.ShapeDtypeStruct((B, B), F32),
@@ -606,8 +619,8 @@
             dma((NP, 2)), dma((2, 3)), dma((NP, 2)), dma((2, 2)),
             dma((10,)), dma((10,)), dma((10, 8)), dma((10,)), dma((10,)),
             dma((2, 8)), dma((16,)), dma((10, 3)), dma((10, 8)), dma((10,)), dma((10, 3)),
-            dma((1,)), dma((2,)), dma((32,)), dma((8, 2)), dma((32,)),
-            dma((7,)), dma((8, 4)), dma((3,)), dma((4, 7)),
+            dma((2,)), dma((2, 2)), dma((8, 4)), dma((8, 2)), dma((8,)), dma((4,)),
+            dma((7,)), dma((8, 4)), dma((3,)), dma((7,)),
         ],
         compiler_params=pltpu.CompilerParams(
             collective_id=1, has_side_effects=True, vmem_limit_bytes=30 * 1024 * 1024),
@@ -623,15 +636,17 @@
     q = p_ref[1]
     acc = jnp.zeros((B, 2 * B), F32)
     for k, b_ref in enumerate((b0, b1, b2, b3)):
-        left = b_ref[0].astype(BF16)
+        left = b_ref[0, 0].astype(BF16)
         acc = acc + dot1(left, whi_ref[k * B:(k + 1) * B, :])
         acc = acc + dot1(left, wlo_ref[k * B:(k + 1) * B, :])
-    m = m_ref[0].astype(F32)
+    m = m_ref[...].astype(F32)
+    m0 = m[:, 0, :]
+    m1 = m[:, 1, :]
     top = (r == 0) & (p < NP)
     factor_col = q < NP
-    c0 = jnp.where(factor_col, acc[:, 0:B], m[:, 0:B] - acc[:, 0:B])
+    c0 = jnp.where(factor_col, acc[:, 0:B], m0 - acc[:, 0:B])
     c0 = jnp.where(top, jnp.where(factor_col, l_ref[...], 0.0), c0)
-    c1 = jnp.where(top, 0.0, m[:, B:] - acc[:, B:])
+    c1 = jnp.where(top, 0.0, m1 - acc[:, B:])
     for n, part in enumerate((c0[:, :128], c0[:, 128:], c1[:, :128], c1[:, 128:])):
         o_ref[pl.ds(n, B, stride=4), :] = part
 
@@ -639,8 +654,8 @@
 def update(place, bulk, mine, whi, wlo, ltile):
     def stream(k):
         def index(r, place):
-            return 8 * (r % 4) + (place[0] + 4 * (r // 4) + k) % 8, 0, 0
-        return pl.BlockSpec((1, B, B), index)
+            return (place[0] + 4 * (r // 4) + k) % 8, r % 4, 0, 0
+        return pl.BlockSpec((1, 1, B, B), index)
 
     return pl.pallas_call(
         update_kernel,
@@ -649,7 +664,7 @@
             num_scalar_prefetch=1,
             grid=(8,),
             in_specs=[stream(k) for k in range(NP)] + [
-                pl.BlockSpec((1, B, 2 * B), lambda r, place: (r, 0, 0)),
+                pl.BlockSpec((B, 2, B), lambda r, place: (r, 0, 0)),
                 pl.BlockSpec((TOP, 2 * B), lambda r, place: (0, 0)),
                 pl.BlockSpec((TOP, 2 * B), lambda r, place: (0, 0)),
                 pl.BlockSpec((B, B), lambda r, place: (0, 0)),
@@ -666,7 +681,7 @@
 def local(covariance):
     mine = covariance.reshape(8, B, 2, B)
     a = mine[0].astype(F32).transpose(1, 0, 2)
-    mine = mine.reshape(8, B, 2 * B)
+    mine = mine.reshape(8 * B, 2, B)
     bulk, whi, wlo, ltile = main(a)
     place = jnp.stack([lax.axis_index("prow"), lax.axis_index("pcol")]).astype(jnp.int32)
     out = update(place, bulk, mine, whi, wlo, ltile)

time: 113 us -> 109 us (0.965); the launches traced: 111 us -> 109 us
  local copies, waits for them, and re-layouts: 4.29 us -> 1.14 us
    another operation x1 -> x0, local copies, waits for them, and re-layouts: 3.16 us -> none  [local(): mine = mine.reshape(8, B, 2 * B)]
where the time goes in v5:
time: 109 us
  Pallas kernels  108 us (99%)
  local copies, waits for them, and re-layouts  1.14 us (1%)
    pallas_call x1, Pallas kernels, main(): pl.pallas_call(main_kernel, out_shape=(jax.ShapeDtypeStruct((8, 4, B, B),...  99.6 us
    pallas_call x1, Pallas kernels, update(): pl.pallas_call(update_kernel, out_shape=jax.ShapeDtypeStruct((8 * 4 * B,...  8.4 us

profile of v5, /device:TPU:9, one launch (start us, length us, event | category | flops | bytes accessed | tf_op | source)
XLA Modules:
  0.0 109.3 jit_solution(13517350888909510539)
XLA Ops:
  0.0 0.1 pad_add_fusion.p_ref
  0.1 1.1 %slice.4 = bf16[1,1,256,2,1,256]{5,3,4,2,1,0:T(2,128)(2,1)S(1)} slice(bf16[8,1,256,2,1,256]{5,3,4,2,1,0:T(2,128)(2,1)} %param.1), slice={[0:1], [0:1], [0:256], [0:2], [0:1], [0:256]} | slice | bytes 524288 | tf_op jit(solution)/shard_map/slice | solution.py:683
  1.3 0.0 copy-start
  1.3 99.6 %main.1 = (f32[8,4,256,256]{3,2,1,0:T(8,128)S(1)}, bf16[1024,512]{1,0:T(8,128)(2,1)S(1)}, bf16[1024,512]{1,0:T(8,128)(2,1)S(1)}, f32[256,256]{1,0:T(8,128)S(1)}) custom-call(f32[2,256,256]{2,1,0:T(8,128)S(1)} %convert_bitcast_fusion.a_ref), custom_call_target="tpu_custom_call" | custom-call | flops 60000002048 | bytes 8000000 | tf_op jit(solution)/shard_map/main/pallas_call | solution.py:602
  100.8 0.0 copy-done
  100.9 8.4 %update.1 = f32[8192,128]{1,0:T(8,128)} custom-call(s32[2]{0:T(128)S(1)} %pad_add_fusion.p_ref, f32[8,4,256,256]{3,2,1,0:T(8,128)S(1)} %get-tuple-element.9.b0.b1.b2.b3, f32[8,4,256,256]{3,2,1,0:T(8,128)S(1)} %get-tuple-element.9.b0.b1.b2.b3, f32[8,4,256,256]{3,2,1,0:T(8,128)S(1)} %get-tuple-element.9.b0.b1.b2.b3, ...), custom_call_target="tpu_custom_call" | custom-call | flops 4300000256 | bytes 16000000 | tf_op jit(solution)/shard_map/update/pallas_call | solution.py:660
  (1 shorter events, 0.0 us)
Async XLA Ops:
  1.3 99.6 %copy-start = (bf16[8,1,256,2,1,256]{5,3,4,2,1,0:T(2,128)(2,1)S(1)}, bf16[8,1,256,2,1,256]{5,3,4,2,1,0:T(2,128)(2,1)}, u32[]{:S(2)}) copy-start(bf16[8,1,256,2,1,256]{5,3,4,2,1,0:T(2,128)(2,1)} %param.1) | copy-start | bytes 6291460

commit v6 on v5

--- a/solution.py
+++ b/solution.py
@@ -630,52 +630,49 @@
     )(a)
 
 
-def update_kernel(p_ref, b0, b1, b2, b3, m_ref, whi_ref, wlo_ref, l_ref, o_ref):
-    r = pl.program_id(0)
+RG = 2
+
+
+def update_kernel(p_ref, b_ref, m_ref, whi_ref, wlo_ref, l_ref, o_ref):
+    first = pl.program_id(0) * RG
     p = p_ref[0]
     q = p_ref[1]
-    acc = jnp.zeros((B, 2 * B), F32)
-    for k, b_ref in enumerate((b0, b1, b2, b3)):
-        left = b_ref[0, 0].astype(BF16)
-        acc = acc + dot1(left, whi_ref[k * B:(k + 1) * B, :])
-        acc = acc + dot1(left, wlo_ref[k * B:(k + 1) * B, :])
-    m = m_ref[...].astype(F32)
-    m0 = m[:, 0, :]
-    m1 = m[:, 1, :]
-    top = (r == 0) & (p < NP)
+
+    def row_tile(r):
+        return jnp.concatenate(
+            [b_ref[(p + 4 * (r // 4) + k) % 8, r % 4].astype(BF16) for k in range(NP)], axis=1)
+
+    left = jnp.concatenate([row_tile(first + n) for n in range(RG)], axis=0)
+    acc = dot1(left, whi_ref[...]) + dot1(left, wlo_ref[...])
     factor_col = q < NP
-    c0 = jnp.where(factor_col, acc[:, 0:B], m0 - acc[:, 0:B])
-    c0 = jnp.where(top, jnp.where(factor_col, l_ref[...], 0.0), c0)
-    c1 = jnp.where(top, 0.0, m1 - acc[:, B:])
-    for n, part in enumerate((c0[:, :128], c0[:, 128:], c1[:, :128], c1[:, 128:])):
-        o_ref[pl.ds(n, B, stride=4), :] = part
+    for n in range(RG):
+        top = (first + n == 0) & (p < NP)
+        m = m_ref[pl.ds(pl.multiple_of((first + n) * B, B), B)].astype(F32)
+        a0 = acc[n * B:(n + 1) * B, 0:B]
+        a1 = acc[n * B:(n + 1) * B, B:]
+        c0 = jnp.where(factor_col, a0, m[:, 0, :] - a0)
+        c0 = jnp.where(top, jnp.where(factor_col, l_ref[...], 0.0), c0)
+        c1 = jnp.where(top, 0.0, m[:, 1, :] - a1)
+        for h, part in enumerate((c0[:, :128], c0[:, 128:], c1[:, :128], c1[:, 128:])):
+            o_ref[pl.ds(4 * B * n + h, B, stride=4), :] = part
 
 
 def update(place, bulk, mine, whi, wlo, ltile):
-    def stream(k):
-        def index(r, place):
-            return (place[0] + 4 * (r // 4) + k) % 8, r % 4, 0, 0
-        return pl.BlockSpec((1, 1, B, B), index)
-
+    vmem = pl.BlockSpec(memory_space=pltpu.VMEM)
     return pl.pallas_call(
         update_kernel,
         out_shape=jax.ShapeDtypeStruct((8 * 4 * B, 128), F32),
         grid_spec=pltpu.PrefetchScalarGridSpec(
             num_scalar_prefetch=1,
-            grid=(8,),
-            in_specs=[stream(k) for k in range(NP)] + [
-                pl.BlockSpec((B, 2, B), lambda r, place: (r, 0, 0)),
-                pl.BlockSpec((TOP, 2 * B), lambda r, place: (0, 0)),
-                pl.BlockSpec((TOP, 2 * B), lambda r, place: (0, 0)),
-                pl.BlockSpec((B, B), lambda r, place: (0, 0)),
-            ],
-            out_specs=pl.BlockSpec((4 * B, 128), lambda r, place: (r, 0)),
+            grid=(8 // RG,),
+            in_specs=[vmem] * 5,
+            out_specs=pl.BlockSpec((4 * B * RG, 128), lambda r, place: (r, 0)),
         ),
-        compiler_params=pltpu.CompilerParams(vmem_limit_bytes=20 * 1024 * 1024),
+        compiler_params=pltpu.CompilerParams(vmem_limit_bytes=24 * 1024 * 1024),
         cost_estimate=pl.CostEstimate(
             flops=4_300_000_000, bytes_accessed=16_000_000, transcendentals=0),
         name="update",
-    )(place, bulk, bulk, bulk, bulk, mine, whi, wlo, ltile)
+    )(place, bulk, mine, whi, wlo, ltile)
 
 
 def local(covariance):

time: 109 us -> 109 us (level)
  no operation moved by 1% of the time
where the time goes in v6:
time: 109 us
  Pallas kernels  108 us (99%)
  local copies, waits for them, and re-layouts  1.14 us (1%)
    pallas_call x1, Pallas kernels, main(): pl.pallas_call(main_kernel, out_shape=(jax.ShapeDtypeStruct((8, 4, B, B),...  99.6 us
    pallas_call x1, Pallas kernels, update(): pl.pallas_call(update_kernel, out_shape=jax.ShapeDtypeStruct((8 * 4 * B,...  8.15 us

profile of v6, /device:TPU:9, one launch (start us, length us, event | category | flops | bytes accessed | tf_op | source)
XLA Modules:
  0.0 109.0 jit_solution(9471671668446146004)
XLA Ops:
  0.0 0.1 pad_add_fusion.p_ref
  0.1 1.1 %slice.4 = bf16[1,1,256,2,1,256]{5,3,4,2,1,0:T(2,128)(2,1)S(1)} slice(bf16[8,1,256,2,1,256]{5,3,4,2,1,0:T(2,128)(2,1)} %param.1), slice={[0:1], [0:1], [0:256], [0:2], [0:1], [0:256]} | slice | bytes 524288 | tf_op jit(solution)/shard_map/slice | solution.py:680
  1.3 0.0 copy-start
  1.3 99.6 %main.1 = (f32[8,4,256,256]{3,2,1,0:T(8,128)S(1)}, bf16[1024,512]{1,0:T(8,128)(2,1)S(1)}, bf16[1024,512]{1,0:T(8,128)(2,1)S(1)}, f32[256,256]{1,0:T(8,128)S(1)}) custom-call(f32[2,256,256]{2,1,0:T(8,128)S(1)} %convert_bitcast_fusion.a_ref), custom_call_target="tpu_custom_call" | custom-call | flops 60000002048 | bytes 8000000 | tf_op jit(solution)/shard_map/main/pallas_call | solution.py:602
  100.8 0.0 copy-done
  100.9 8.2 %update.1 = f32[8192,128]{1,0:T(8,128)} custom-call(s32[2]{0:T(128)S(1)} %pad_add_fusion.p_ref, f32[8,4,256,256]{3,2,1,0:T(8,128)S(1)} %get-tuple-element.9.b_ref, bf16[2048,2,256]{2,1,0:T(2,128)(2,1)S(1)} %bitcast.11, bf16[1024,512]{1,0:T(8,128)(2,1)S(1)} %get-tuple-element.10.whi_ref, bf16[1024,512]{1,0:T(8,128)(2,1)S(1)} %get-tuple-element.11.wlo_ref, ...), custom_call_target="tpu_custom_call" | custom-call | flops 4300000256 | bytes 16000000 | tf_op jit(solution)/shard_map/update/pallas_call | solution.py:662
  (1 shorter events, 0.0 us)
Async XLA Ops:
  1.3 99.6 %copy-start = (bf16[8,1,256,2,1,256]{5,3,4,2,1,0:T(2,128)(2,1)S(1)}, bf16[8,1,256,2,1,256]{5,3,4,2,1,0:T(2,128)(2,1)}, u32[]{:S(2)}) copy-start(bf16[8,1,256,2,1,256]{5,3,4,2,1,0:T(2,128)(2,1)} %param.1) | copy-start | bytes 6291460

commit v7 on v6

--- a/solution.py
+++ b/solution.py
@@ -630,7 +630,7 @@
     )(a)
 
 
-RG = 2
+RG = 4
 
 
 def update_kernel(p_ref, b_ref, m_ref, whi_ref, wlo_ref, l_ref, o_ref):

time: 109 us -> 109 us (level)
  no operation moved by 1% of the time
where the time goes in v7:
time: 109 us
  Pallas kernels  108 us (99%)
  local copies, waits for them, and re-layouts  1.14 us (1%)
    pallas_call x1, Pallas kernels, main(): pl.pallas_call(main_kernel, out_shape=(jax.ShapeDtypeStruct((8, 4, B, B),...  99.6 us
    pallas_call x1, Pallas kernels, update(): pl.pallas_call(update_kernel, out_shape=jax.ShapeDtypeStruct((8 * 4 * B,...  8.28 us

profile of v7, /device:TPU:9, one launch (start us, length us, event | category | flops | bytes accessed | tf_op | source)
XLA Modules:
  0.0 109.1 jit_solution(10117988398171213965)
XLA Ops:
  0.0 0.1 pad_add_fusion.p_ref
  0.1 1.1 %slice.4 = bf16[1,1,256,2,1,256]{5,3,4,2,1,0:T(2,128)(2,1)S(1)} slice(bf16[8,1,256,2,1,256]{5,3,4,2,1,0:T(2,128)(2,1)} %param.1), slice={[0:1], [0:1], [0:256], [0:2], [0:1], [0:256]} | slice | bytes 524288 | tf_op jit(solution)/shard_map/slice | solution.py:680
  1.3 0.0 copy-start
  1.3 99.6 %main.1 = (f32[8,4,256,256]{3,2,1,0:T(8,128)S(1)}, bf16[1024,512]{1,0:T(8,128)(2,1)S(1)}, bf16[1024,512]{1,0:T(8,128)(2,1)S(1)}, f32[256,256]{1,0:T(8,128)S(1)}) custom-call(f32[2,256,256]{2,1,0:T(8,128)S(1)} %convert_bitcast_fusion.a_ref), custom_call_target="tpu_custom_call" | custom-call | flops 60000002048 | bytes 8000000 | tf_op jit(solution)/shard_map/main/pallas_call | solution.py:602
  100.8 0.0 copy-done
  100.9 8.3 %update.1 = f32[8192,128]{1,0:T(8,128)} custom-call(s32[2]{0:T(128)S(1)} %pad_add_fusion.p_ref, f32[8,4,256,256]{3,2,1,0:T(8,128)S(1)} %get-tuple-element.9.b_ref, bf16[2048,2,256]{2,1,0:T(2,128)(2,1)S(1)} %bitcast.11, bf16[1024,512]{1,0:T(8,128)(2,1)S(1)} %get-tuple-element.10.whi_ref, bf16[1024,512]{1,0:T(8,128)(2,1)S(1)} %get-tuple-element.11.wlo_ref, ...), custom_call_target="tpu_custom_call" | custom-call | flops 4300000256 | bytes 16000000 | tf_op jit(solution)/shard_map/update/pallas_call | solution.py:662
  (1 shorter events, 0.0 us)
Async XLA Ops:
  1.3 99.6 %copy-start = (bf16[8,1,256,2,1,256]{5,3,4,2,1,0:T(2,128)(2,1)S(1)}, bf16[8,1,256,2,1,256]{5,3,4,2,1,0:T(2,128)(2,1)}, u32[]{:S(2)}) copy-start(bf16[8,1,256,2,1,256]{5,3,4,2,1,0:T(2,128)(2,1)} %param.1) | copy-start | bytes 6291460
